TPU v7x, 256 devices: a whole 4x4x8 slice. The times are simulated.
256 devices in a mesh: section: 4 (over y), dp: 2 (over x_hi), tensor: 32 (over x_lo, z, core).
Axes of the slice: x: 4 (x_hi: 2, x_lo: 2; x = x_hi * 2 + x_lo), y: 4, z: 8, core: 2. Of those that a mesh axis runs over, the one named last changes fastest.
Arguments:
- weights: bfloat16 [4, 6144, 24576], P('section', 'dp', 'tensor'), may hold values from -0.078125 to 0.078125
- arriving: bfloat16 [4, 2, 512, 6144], P('section', None, ('dp', 'tensor')), may hold values from -50 to 50
- vectors: float32 [4, 6144], P('section'), may hold values from 0.25 to 1.75
Outputs:
- leaving: bfloat16 [4, 2, 512, 6144], P('section', None, ('dp', 'tensor'))
- weight_grads: bfloat16 [4, 6144, 24576], P('section', 'dp', 'tensor')
- vector_grads: float32 [4, 6144], P('section')
All inputs are finite; a program needn't handle non-finite values.
Results may differ from a plain program's by a relative error of at most 0.024.
Values may be sent and summed in bfloat16 or wider, within the bound.
A program may use at most 128 MiB of HBM per device.

v0:
```python
import jax
import jax.numpy as jnp
from jax import lax
from jax.sharding import PartitionSpec as P

coeff = 0.7978845608028654


def from_partner(block, axis, bit):
    count = lax.axis_size(axis)
    route = []
    for low in range(count):
        high = low | 1 << bit
        if high != low and high < count:
            route += [(low, high), (high, low)]
    return lax.ppermute(block, axis, route)


def gelu_value(inputs):
    inner = jnp.tanh(coeff * (inputs + 0.044715 * inputs * inputs * inputs))
    return 0.5 * inputs * (1.0 + inner)


def gelu_slope(inputs):
    inner = jnp.tanh(coeff * (inputs + 0.044715 * inputs * inputs * inputs))
    return 0.5 * (1.0 + inner) + 0.5 * inputs * (1.0 - inner * inner) * coeff * (
        1.0 + 3.0 * 0.044715 * inputs * inputs
    )


def local(weights, arriving, vectors):
    leading = lax.axis_index("section") % 2 == 0
    local_weight = weights[0]
    weight_full = lax.all_gather(weights, "dp", axis=1, tiled=True)[0]
    hidden_width = local_weight.shape[1]
    section_vec = vectors[0]
    stream = arriving[0]
    model_width = stream.shape[2]
    values = stream.astype(jnp.float32)
    centred = values - jnp.mean(values, axis=-1, keepdims=True)
    scaled = lax.rsqrt(jnp.mean(centred * centred, axis=-1, keepdims=True) + 1e-05)
    standard = centred * scaled
    normed = (standard * section_vec).astype(jnp.bfloat16)
    outgoing = jnp.where(leading, normed, stream)

    def handle(offset, amount):
        own_rows = outgoing[offset : offset + amount]
        gathered = lax.all_gather(own_rows, "tensor", axis=1, tiled=True)
        tokens = gathered.shape[1]
        row_inputs = gathered.reshape(amount * tokens, model_width)
        preact = jnp.dot(row_inputs, weight_full, preferred_element_type=jnp.float32)
        outbound = jnp.where(leading, gelu_value(preact), preact).astype(jnp.bfloat16)
        outbound = outbound.reshape(amount, tokens, hidden_width)
        back_hidden, back_rows = from_partner(
            (outbound, stream[offset : offset + amount]), "section", 0
        )
        gelu_grad = gelu_slope(preact).reshape(amount, tokens, hidden_width)
        carried = jnp.where(
            leading, (back_hidden.astype(jnp.float32) * gelu_grad).astype(jnp.bfloat16), back_hidden
        )
        summed = lax.psum_scatter(
            jnp.einsum(
                "kaf,df->akd", carried, weight_full, preferred_element_type=jnp.float32
            ).astype(jnp.bfloat16),
            "tensor",
            scatter_dimension=0,
            tiled=True,
        ).astype(jnp.float32)
        summed = jnp.transpose(summed, (1, 0, 2))
        hidden_inputs = carried.reshape(amount * tokens, hidden_width)
        residual = back_rows.astype(jnp.float32)
        piece_std = standard[offset : offset + amount]
        piece_scale = scaled[offset : offset + amount]
        grad_norm = summed * section_vec
        mean_grad = jnp.mean(grad_norm, axis=-1, keepdims=True)
        mean_mix = jnp.mean(grad_norm * piece_std, axis=-1, keepdims=True)
        through = (grad_norm - mean_grad - piece_std * mean_mix) * piece_scale
        result_rows = jnp.where(
            leading, residual + through, residual + summed + section_vec
        ).astype(jnp.bfloat16)
        vector_term = jnp.where(
            leading,
            jnp.sum(summed * piece_std, axis=(0, 1)),
            jnp.sum(values[offset : offset + amount], axis=(0, 1)),
        )
        return (result_rows, vector_term, row_inputs, hidden_inputs)

    results = [handle(micro_index, 1) for micro_index in range(stream.shape[0])]
    leaving = jnp.concatenate([entry[0] for entry in results], axis=0)
    vector_total = results[0][1]
    for entry in results[1:]:
        vector_total = vector_total + entry[1]
    row_all = jnp.concatenate([entry[2] for entry in results], axis=0)
    hidden_all = jnp.concatenate([entry[3] for entry in results], axis=0)
    weight_grad = lax.psum_scatter(
        lax.dot_general(
            row_all, hidden_all, (((0,), (0,)), ((), ())), preferred_element_type=jnp.float32
        ).astype(jnp.bfloat16),
        "dp",
        scatter_dimension=0,
        tiled=True,
    )
    totals = lax.psum(vector_total, ("dp", "tensor"))
    return (leaving[None], weight_grad[None], totals[None])


def solution(mesh):
    placed = (
        P("section", "dp", "tensor"),
        P("section", None, ("dp", "tensor"), None),
        P("section", None),
    )
    return jax.shard_map(
        local,
        mesh=mesh,
        in_specs=placed,
        out_specs=(
            P("section", None, ("dp", "tensor"), None),
            P("section", "dp", "tensor"),
            P("section", None),
        ),
        check_vma=False,
    )
```

profile of v0, /device:TPU:1, one launch (start us, length us, event | category | flops | bytes accessed | tf_op | source)
XLA Modules:
  0.0 770.6 jit_solution(1868036535329829601)
XLA Ops:
  7.2 1.1 convert_reduce_fusion
  8.3 1.1 multiply_reduce_fusion
  9.4 1.1 fusion.68
  10.5 0.7 fusion.72
  11.3 0.7 all-gather.6.cloned.1.call-update
  12.0 0.7 all-gather.4.cloned.1.call-update
  12.8 69.0 %all-gather.8.cloned.1.call-done = bf16[1,256,6144]{2,1,0:T(8,128)(2,1)} async-done(((bf16[1,8,6144]{2,1,0:T(8,128)(2,1)}), bf16[1,256,6144]{2,1,0:T(8,128)(2,1)}) %all-gather.8.cloned.1.call-update) | async-done | bytes 3145744 | tf_op jit(solution)/shard_map/all_gather | solution.py:48
  81.7 125.6 %all-gather.6.cloned.1.call-done = bf16[1,6144,768]{2,1,0:T(8,128)(2,1)} async-done(((bf16[1,3072,768]{2,1,0:T(8,128)(2,1)}), bf16[1,6144,768]{2,1,0:T(8,128)(2,1)}) %all-gather.6.cloned.1.call-update) | async-done | bytes 9437200 | tf_op jit(solution)/shard_map/all_gather | solution.py:34
  207.4 7.4 fusion.2
  214.7 0.3 fusion.45
  215.0 1.3 collective-permute-start.3
  216.3 8.8 %collective-permute-done.3 = bf16[1,256,768]{2,1,0:T(8,128)(2,1)S(1)} collective-permute-done((bf16[1,256,768]{2,1,0:T(8,128)(2,1)S(1)}, bf16[1,256,768]{2,1,0:T(8,128)(2,1)S(1)}, u32[]{:S(2)}, u32[]{:S(2)}) %collective-permute-start.3) | collective-permute-done | bytes 393248 | tf_op jit(solution)/shard_map/ppermute | solution.py:16
  225.1 0.6 fusion.47
  225.7 4.1 fusion.14
  229.8 46.0 %all-gather.4.cloned.1.call-done = bf16[1,256,6144]{2,1,0:T(8,128)(2,1)} async-done(((bf16[1,8,6144]{2,1,0:T(8,128)(2,1)}), bf16[1,256,6144]{2,1,0:T(8,128)(2,1)}) %all-gather.4.cloned.1.call-update) | async-done | bytes 3145744 | tf_op jit(solution)/shard_map/all_gather | solution.py:48
  275.8 7.2 fusion.6
  283.1 0.3 fusion.44
  283.4 1.3 collective-permute-start.1
  284.7 9.3 %collective-permute-done.1 = bf16[1,256,768]{2,1,0:T(8,128)(2,1)S(1)} collective-permute-done((bf16[1,256,768]{2,1,0:T(8,128)(2,1)S(1)}, bf16[1,256,768]{2,1,0:T(8,128)(2,1)S(1)}, u32[]{:S(2)}, u32[]{:S(2)}) %collective-permute-start.1) | collective-permute-done | bytes 393248 | tf_op jit(solution)/shard_map/ppermute | solution.py:16
  294.0 0.6 fusion.46
  294.5 11.2 %fusion.17 = bf16[256,1,6144]{2,0,1:T(8,128)(2,1)} fusion(bf16[256,768]{1,0:T(8,128)(2,1)S(1)} %fusion.46, bf16[1,6144,768]{2,1,0:T(8,128)(2,1)} %all-gather.6.cloned.1.call-done), kind=kOutput, calls=%fused_computation.12 | convolution fusion | flops 2417491968 | bytes 12976128 | tf_op jit(solution)/shard_map/kaf,df->akd/dot_general | solution.py:62
  305.8 0.2 reduce-scatter.8.cloned.1.call-start
  306.0 12.1 %convolution_convert_fusion = bf16[6144,768]{1,0:T(8,128)(2,1)} fusion(bf16[256,6144]{1,0:T(8,128)(2,1)} %bitcast.103, bf16[256,6144]{1,0:T(8,128)(2,1)} %bitcast.104, bf16[256,768]{1,0:T(8,128)(2,1)S(1)} %fusion.47, bf16[256,768]{1,0:T(8,128)(2,1)S(1)} %fusion.46), kind=kOutput, calls=%fused_computation | convolution fusion | flops 4850712576 | bytes 16515072 | tf_op jit(solution)/shard_map/dot_general | solution.py:96
  318.1 0.9 copy-done
  319.1 1.3 collective-permute-start
  320.3 0.3 collective-permute-start.2
  320.9 72.8 %reduce-scatter.6.cloned.1.call-done = bf16[8,1,6144]{2,0,1:T(8,128)(2,1)} async-done(((bf16[256,1,6144]{2,0,1:T(8,128)(2,1)}), bf16[8,1,6144]{2,0,1:T(8,128)(2,1)}) %reduce-scatter.6.cloned.1.call-update) | async-done | bytes 98320 | tf_op jit(solution)/shard_map/reduce_scatter | solution.py:61
  393.7 118.8 %reduce-scatter.4.cloned.1.call-done = bf16[8,1,6144]{2,0,1:T(8,128)(2,1)} async-done(((bf16[256,1,6144]{2,0,1:T(8,128)(2,1)}), bf16[8,1,6144]{2,0,1:T(8,128)(2,1)}) %reduce-scatter.4.cloned.1.call-update) | async-done | bytes 98320 | tf_op jit(solution)/shard_map/reduce_scatter | solution.py:61
  512.5 1.3 fusion.67
  513.8 248.1 %psum.7 = f32[1,6144]{1,0:T(1,128)} all-reduce(f32[1,6144]{1,0:T(1,128)S(1)} %bitcast.101), channel_id=1, replica_groups=mesh['section'=4,'dp'=2,'tensor'=32] {'dp','tensor'}, use_global_device_ids=true, to_apply=%region_13.14 | all-reduce | flops 6144 | bytes 49152 | tf_op jit(solution)/shard_map/psum | solution.py:103
  761.9 1.1 fusion.55
  763.1 0.7 maximum_bitcast_fusion
  (27 shorter events, 0.6 us)
Async XLA Ops:
  7.2 74.6 %all-gather.8.cloned.1.call-start = ((), (), s32[]{:S(2)}) async-start(), calls=%async_computation.6 | async-start | bytes 3244032 | tf_op jit(solution)/shard_map/all_gather | solution.py:48
  11.2 196.1 %all-gather.6.cloned.1.call-start = ((), (), s32[]{:S(2)}) async-start(), calls=%async_computation.4 | async-start | bytes 14155776 | tf_op jit(solution)/shard_map/all_gather | solution.py:34
  12.0 263.9 %all-gather.4.cloned.1.call-start = ((), (), s32[]{:S(2)}) async-start(), calls=%async_computation.3 | async-start | bytes 3244032 | tf_op jit(solution)/shard_map/all_gather | solution.py:48
  12.7 381.0 %reduce-scatter.6.cloned.1.call-start = ((), (), s32[]{:S(2)}) async-start(), calls=%async_computation.7 | async-start | bytes 3244032 | tf_op jit(solution)/shard_map/reduce_scatter | solution.py:61
  207.4 18.3 %copy-start.2 = (bf16[1,6144,768]{2,1,0:T(8,128)(2,1)S(1)}, bf16[1,6144,768]{2,1,0:T(8,128)(2,1)}, u32[]{:S(2)}) copy-start(bf16[1,6144,768]{2,1,0:T(8,128)(2,1)} %all-gather.6.cloned.1.call-done) | copy-start | bytes 28311556
  215.0 10.1 %collective-permute-start.3 = (bf16[1,256,768]{2,1,0:T(8,128)(2,1)S(1)}, bf16[1,256,768]{2,1,0:T(8,128)(2,1)S(1)}, u32[]{:S(2)}, u32[]{:S(2)}) collective-permute-start(bf16[1,256,768]{2,1,0:T(8,128)(2,1)S(1)} %fusion.45), channel_id=1, source_target_pairs={{0,64},{64,0},{128,192},{192,128},{1,65},{65,1},{129,193},{193,129... | collective-permute-start | bytes 1179656 | tf_op jit(solution)/shard_map/ppermute | solution.py:16
  229.8 282.7 %reduce-scatter.4.cloned.1.call-start = ((), (), s32[]{:S(2)}) async-start(), calls=%async_computation.5 | async-start | bytes 3244032 | tf_op jit(solution)/shard_map/reduce_scatter | solution.py:61
  283.4 10.6 %collective-permute-start.1 = (bf16[1,256,768]{2,1,0:T(8,128)(2,1)S(1)}, bf16[1,256,768]{2,1,0:T(8,128)(2,1)S(1)}, u32[]{:S(2)}, u32[]{:S(2)}) collective-permute-start(bf16[1,256,768]{2,1,0:T(8,128)(2,1)S(1)} %fusion.44), channel_id=1, source_target_pairs={{0,64},{64,0},{128,192},{192,128},{1,65},{65,1},{129,193},{193,129... | collective-permute-start | bytes 1179656 | tf_op jit(solution)/shard_map/ppermute | solution.py:16
  305.8 458.0 %reduce-scatter.8.cloned.1.call-start = ((), (), s32[]{:S(2)}) async-start(), calls=%async_computation.8 | async-start | bytes 14155776 | tf_op jit(solution)/shard_map/reduce_scatter | solution.py:95
  318.1 0.9 copy-start
  318.1 194.4 %copy-start.1 = (f32[1,6144]{1,0:T(1,128)S(1)}, f32[1,6144]{1,0:T(1,128)}, u32[]{:S(2)}) copy-start(f32[1,6144]{1,0:T(1,128)} %param.5) | copy-start | bytes 73732
  319.1 442.9 %collective-permute-start = (bf16[1,8,6144]{2,1,0:T(8,128)(2,1)S(1)}, bf16[1,8,6144]{2,1,0:T(8,128)(2,1)S(1)}, u32[]{:S(2)}, u32[]{:S(2)}) collective-permute-start(bf16[1,8,6144]{2,1,0:T(8,128)(2,1)S(1)} %get-tuple-element.15), channel_id=1, source_target_pairs={{0,64},{64,0},{128,192},{192,128},{1,65},{65,1},{129,193},{193,129... | collective-permute-start | bytes 294920 | tf_op jit(solution)/shard_map/ppermute | solution.py:16
  320.3 441.6 %collective-permute-start.2 = (bf16[1,8,6144]{2,1,0:T(8,128)(2,1)S(1)}, bf16[1,8,6144]{2,1,0:T(8,128)(2,1)S(1)}, u32[]{:S(2)}, u32[]{:S(2)}) collective-permute-start(bf16[1,8,6144]{2,1,0:T(8,128)(2,1)S(1)} %get-tuple-element.16), channel_id=1, source_target_pairs={{0,64},{64,0},{128,192},{192,128},{1,65},{65,1},{129,193},{193,129... | collective-permute-start | bytes 294920 | tf_op jit(solution)/shard_map/ppermute | solution.py:16
Sparse Core Ops, SparseCore 0:
  11.4 70.3 all-gather.7
  83.5 123.7 all-gather.5
  209.8 65.9 all-gather.3
  278.2 115.4 reduce-scatter.5
  396.2 116.2 reduce-scatter.3
  515.5 118.5 reduce-scatter.7
where the time goes:
time: 775 us; the launch traced here: 771 us
  waiting for transfers between devices  452 us (58%)
  blocking collectives  248 us (32%)
  matrix products  42 us (5%)
  between operations  14.2 us (2%)
  other arithmetic  8.3 us (1%)
    psum x1, blocking collectives, local(): totals = lax.psum(vector_total, ('dp', 'tensor'))  248 us
    reduce_scatter x2, waiting for transfers between devices, handle(): lax.psum_scatter(jnp.einsum('kaf,df->akd', carried, weight_full, preferre...  192 us
    all_gather x1, waiting for transfers between devices, local(): weight_full = lax.all_gather(weights, 'dp', axis=1, tiled=True)[0]  126 us
    all_gather x2, waiting for transfers between devices, handle(): gathered = lax.all_gather(own_rows, 'tensor', axis=1, tiled=True)  115 us
    ppermute x4, waiting for transfers between devices, from_partner(): return lax.ppermute(block, axis, route)  18.1 us
  transfers between devices with their start and end apart: 10, of which 7 were waited for; matrix products, arithmetic and copies ran while one was open for 6% of the time, Pallas kernels for 0%

commit v1 on v0

v1 whole, which is shorter than its diff:
```python
import jax
import jax.numpy as jnp
from jax import lax
from jax.sharding import PartitionSpec as P

coeff = 0.7978845608028654


def swap(block, axis):
    count = lax.axis_size(axis)
    return lax.ppermute(block, axis, [(i, i ^ 1) for i in range(count)])


def gelu_value(inputs):
    inner = jnp.tanh(coeff * (inputs + 0.044715 * inputs * inputs * inputs))
    return 0.5 * inputs * (1.0 + inner)


def gelu_slope(inputs):
    inner = jnp.tanh(coeff * (inputs + 0.044715 * inputs * inputs * inputs))
    return 0.5 * (1.0 + inner) + 0.5 * inputs * (1.0 - inner * inner) * coeff * (
        1.0 + 3.0 * 0.044715 * inputs * inputs
    )


def local(weights, arriving, vectors):
    leading = lax.axis_index("section") % 2 == 0
    replica = lax.axis_index("dp")
    weight = weights[0]
    half, width = weight.shape
    gain = vectors[0]
    stream = arriving[0]
    micro, rows, model = stream.shape
    values = stream.astype(jnp.float32)
    centred = values - jnp.mean(values, axis=-1, keepdims=True)
    scaled = lax.rsqrt(jnp.mean(centred * centred, axis=-1, keepdims=True) + 1e-05)
    standard = centred * scaled
    normed = (standard * gain).astype(jnp.bfloat16)
    outgoing = jnp.where(leading, normed, stream)
    back_rows = swap(stream, "section")

    def split(block, index):
        return lax.dynamic_slice_in_dim(block, index * half, half, block.ndim - 1)

    kept = split(outgoing, replica)
    came = swap(split(outgoing, 1 - replica), "dp")
    sums, gathers, carries = [], [], []
    for m in range(micro):
        pair = jnp.concatenate([kept[m], came[m]], axis=0)
        gathered = lax.all_gather(pair, "tensor", axis=0, tiled=True)
        gathered = gathered.reshape(-1, 2, rows, half)
        first = gathered[:, 0]
        second = gathered[:, 1]
        gathered = jnp.concatenate(
            [jnp.where(replica == 0, first, second), jnp.where(replica == 0, second, first)], axis=0
        ).reshape(-1, half)
        partial = jnp.dot(gathered, weight, preferred_element_type=jnp.float32)
        preact = partial + swap(partial.astype(jnp.bfloat16), "dp").astype(jnp.float32)
        outbound = jnp.where(leading, gelu_value(preact), preact).astype(jnp.bfloat16)
        back_hidden = swap(outbound, "section")
        carried = jnp.where(
            leading,
            (back_hidden.astype(jnp.float32) * gelu_slope(preact)).astype(jnp.bfloat16),
            back_hidden,
        )
        product = lax.dot_general(
            carried, weight, (((1,), (1,)), ((), ())), preferred_element_type=jnp.float32
        ).astype(jnp.bfloat16)
        product = jnp.transpose(product.reshape(2, -1, rows, half), (1, 0, 2, 3)).reshape(-1, half)
        total = lax.psum_scatter(product, "tensor", scatter_dimension=0, tiled=True)
        sums.append(total.reshape(2, rows, half))
        gathers.append(gathered)
        carries.append(carried)
    total = jnp.stack(sums, axis=1)
    mine = lax.dynamic_index_in_dim(total, replica, 0, False)
    theirs = swap(lax.dynamic_index_in_dim(total, 1 - replica, 0, False), "dp")
    summed = jnp.concatenate(
        [jnp.where(replica == 0, mine, theirs), jnp.where(replica == 0, theirs, mine)], axis=-1
    ).astype(jnp.float32)
    grad_norm = summed * gain
    mean_grad = jnp.mean(grad_norm, axis=-1, keepdims=True)
    mean_mix = jnp.mean(grad_norm * standard, axis=-1, keepdims=True)
    through = (grad_norm - mean_grad - standard * mean_mix) * scaled
    residual = back_rows.astype(jnp.float32)
    leaving = jnp.where(leading, residual + through, residual + summed + gain).astype(jnp.bfloat16)
    vector_term = jnp.where(
        leading, jnp.sum(summed * standard, axis=(0, 1)), jnp.sum(values, axis=(0, 1))
    )
    weight_grad = lax.dot_general(
        jnp.concatenate(gathers, axis=0),
        jnp.concatenate(carries, axis=0),
        (((0,), (0,)), ((), ())),
        preferred_element_type=jnp.float32,
    ).astype(jnp.bfloat16)
    totals = lax.psum(vector_term, ("dp", "tensor"))
    return (leaving[None], weight_grad[None], totals[None])


def solution(mesh):
    placed = (
        P("section", "dp", "tensor"),
        P("section", None, ("dp", "tensor"), None),
        P("section", None),
    )
    return jax.shard_map(
        local,
        mesh=mesh,
        in_specs=placed,
        out_specs=(
            P("section", None, ("dp", "tensor"), None),
            P("section", "dp", "tensor"),
            P("section", None),
        ),
        check_vma=False,
    )
```

time: 775 us -> 664 us (0.86)
  waiting for transfers between devices: 452 us -> 334 us
  matrix products: 42 us -> 23.6 us
  other arithmetic: 8.3 us -> 20 us
  starting transfers between devices: 4.56 us -> 15.1 us
    all_gather x3 -> x2, waiting for transfers between devices: 241 us -> 80.7 us  [local(): gathered = lax.all_gather(pair, 'tensor', axis=0, tiled=True)]
    ppermute x4 -> x7, waiting for transfers between devices: 18.1 us -> 77.8 us  [swap(): return lax.ppermute(block, axis, [(i, i ^ 1) for i in range(count)])]
    dot_general x5, matrix products: 42 us -> 23.6 us  [the longest x1 9.15 us: local(): lax.dot_general(jnp.concatenate(gathers, axis=0), jnp.concatenate(carries...]
    reduce_scatter x3 -> x2, waiting for transfers between devices: 192 us -> 176 us  [local(): total = lax.psum_scatter(product, 'tensor', scatter_dimension=0, tiled=True)]
    ppermute x4 -> x7, starting transfers between devices: 4.14 us -> 14.9 us  [swap(): return lax.ppermute(block, axis, [(i, i ^ 1) for i in range(count)])]
  transfers between devices with their start and end apart: 10 -> 11, of which waited for: 7 -> 9; matrix products, arithmetic and copies ran while one was open for 6% -> 6% of each run, Pallas kernels for 0% -> 0%
where the time goes in v1:
time: 664 us; the launch traced here: 660 us
  waiting for transfers between devices  334 us (50%)
  blocking collectives  245 us (37%)
  matrix products  23.6 us (4%)
  other arithmetic  20 us (3%)
  starting transfers between devices  15.1 us (2%)
  between operations  14 us (2%)
  local copies, waits for them, and re-layouts  7.51 us (1%)
    psum x1, blocking collectives, local(): totals = lax.psum(vector_term, ('dp', 'tensor'))  245 us
    reduce_scatter x2, waiting for transfers between devices, local(): total = lax.psum_scatter(product, 'tensor', scatter_dimension=0, tiled=True)  176 us
    all_gather x2, waiting for transfers between devices, local(): gathered = lax.all_gather(pair, 'tensor', axis=0, tiled=True)  80.7 us
    ppermute x7, waiting for transfers between devices, swap(): return lax.ppermute(block, axis, [(i, i ^ 1) for i in range(count)])  77.8 us
    ppermute x7, starting transfers between devices, swap(): return lax.ppermute(block, axis, [(i, i ^ 1) for i in range(count)])  14.9 us
  transfers between devices with their start and end apart: 11, of which 9 were waited for; matrix products, arithmetic and copies ran while one was open for 6% of the time, Pallas kernels for 0%

profile of v1, /device:TPU:1, one launch (start us, length us, event | category | flops | bytes accessed | tf_op | source)
XLA Modules:
  0.0 660.1 jit_solution(4978128048869185818)
XLA Ops:
  7.2 1.7 convert_reduce_fusion
  8.9 1.1 fusion.55
  11.2 3.7 collective-permute-start.1
  14.8 2.0 collective-permute-done.1
  18.3 70.2 %all-gather.5.cloned.1.call-done = bf16[512,3072]{1,0:T(8,128)(2,1)} async-done(((bf16[16,3072]{1,0:T(8,128)(2,1)}), bf16[512,3072]{1,0:T(8,128)(2,1)}) %all-gather.5.cloned.1.call-update) | async-done | bytes 3145744 | tf_op jit(solution)/shard_map/all_gather | solution.py:50
  88.5 2.2 fusion.38
  91.6 2.2 copy-done.10
  93.7 2.6 fusion.69
  96.4 2.5 collective-permute-start.4
  98.9 23.2 %collective-permute-done.4 = bf16[512,768]{1,0:T(8,128)(2,1)S(1)} collective-permute-done((bf16[512,768]{1,0:T(8,128)(2,1)S(1)}, bf16[512,768]{1,0:T(8,128)(2,1)S(1)}, u32[]{:S(2)}, u32[]{:S(2)}) %collective-permute-start.4) | collective-permute-done | bytes 786464 | tf_op jit(solution)/shard_map/ppermute | solution.py:11
  122.7 1.3 collective-permute-start.5
  124.0 16.1 %collective-permute-done.5 = bf16[512,768]{1,0:T(8,128)(2,1)S(1)} collective-permute-done((bf16[512,768]{1,0:T(8,128)(2,1)S(1)}, bf16[512,768]{1,0:T(8,128)(2,1)S(1)}, u32[]{:S(2)}, u32[]{:S(2)}) %collective-permute-start.5) | collective-permute-done | bytes 786464 | tf_op jit(solution)/shard_map/ppermute | solution.py:11
  140.1 1.2 fusion.43
  141.3 2.9 fusion.21
  144.2 1.9 copy.19
  146.1 10.4 %all-gather.3.cloned.1.call-done = bf16[512,3072]{1,0:T(8,128)(2,1)} async-done(((bf16[16,3072]{1,0:T(8,128)(2,1)}), bf16[512,3072]{1,0:T(8,128)(2,1)}) %all-gather.3.cloned.1.call-update) | async-done | bytes 3145744 | tf_op jit(solution)/shard_map/all_gather | solution.py:50
  156.6 2.2 select_bitcast_fusion.1
  158.9 6.1 fusion.68
  164.9 2.7 collective-permute-start.2
  167.6 19.9 %collective-permute-done.2 = bf16[512,768]{1,0:T(8,128)(2,1)S(1)} collective-permute-done((bf16[512,768]{1,0:T(8,128)(2,1)S(1)}, bf16[512,768]{1,0:T(8,128)(2,1)S(1)}, u32[]{:S(2)}, u32[]{:S(2)}) %collective-permute-start.2) | collective-permute-done | bytes 786464 | tf_op jit(solution)/shard_map/ppermute | solution.py:11
  188.2 1.5 collective-permute-start.3
  189.6 16.7 %collective-permute-done.3 = bf16[512,768]{1,0:T(8,128)(2,1)S(1)} collective-permute-done((bf16[512,768]{1,0:T(8,128)(2,1)S(1)}, bf16[512,768]{1,0:T(8,128)(2,1)S(1)}, u32[]{:S(2)}, u32[]{:S(2)}) %collective-permute-start.3) | collective-permute-done | bytes 786464 | tf_op jit(solution)/shard_map/ppermute | solution.py:11
  206.4 1.2 fusion.44
  207.6 2.9 fusion.18
  210.5 1.9 copy.14
  213.3 1.2 collective-permute-start
  214.6 4.4 maximum_bitcast_fusion
  219.0 56.5 %reduce-scatter.5.cloned.1.call-done = bf16[16,3072]{1,0:T(8,128)(2,1)} async-done(((bf16[512,3072]{1,0:T(8,128)(2,1)}), bf16[16,3072]{1,0:T(8,128)(2,1)}) %reduce-scatter.5.cloned.1.call-update) | async-done | bytes 98320 | tf_op jit(solution)/shard_map/reduce_scatter | solution.py:70
  275.5 119.2 %reduce-scatter.3.cloned.1.call-done = bf16[16,3072]{1,0:T(8,128)(2,1)} async-done(((bf16[512,3072]{1,0:T(8,128)(2,1)}), bf16[16,3072]{1,0:T(8,128)(2,1)}) %reduce-scatter.3.cloned.1.call-update) | async-done | bytes 98320 | tf_op jit(solution)/shard_map/reduce_scatter | solution.py:70
  395.5 2.1 collective-permute-start.6
  397.6 9.1 %fusion.15 = bf16[1,3072,768]{2,1,0:T(8,128)(2,1)} fusion(bf16[512,3072]{1,0:T(8,128)(2,1)} %get-tuple-element.23, bf16[512,3072]{1,0:T(8,128)(2,1)} %get-tuple-element.22, bf16[512,768]{1,0:T(8,128)(2,1)} %copy-done.4, bf16[512,768]{1,0:T(8,128)(2,1)} %copy-done.5), kind=kOutput, calls=%fused_computation.13 | convolution fusion | flops 4849926144 | bytes 12582912 | tf_op jit(solution)/shard_map/dot_general | solution.py:89
  407.1 245.5 %psum.7 = f32[1,6144]{1,0:T(1,128)} all-reduce(f32[1,6144]{1,0:T(1,128)S(1)} %bitcast.118), channel_id=1, replica_groups=mesh['section'=4,'dp'=2,'tensor'=32] {'dp','tensor'}, use_global_device_ids=true, to_apply=%region_8.9 | all-reduce | flops 6144 | bytes 49152 | tf_op jit(solution)/shard_map/psum | solution.py:95
  (53 shorter events, 7.8 us)
Async XLA Ops:
  7.2 81.4 %all-gather.5.cloned.1.call-start = ((), (), s32[]{:S(2)}) async-start(), calls=%async_computation.4 | async-start | bytes 3244032 | tf_op jit(solution)/shard_map/all_gather | solution.py:50
  11.2 5.7 collective-permute-start.1
  17.5 139.1 %all-gather.3.cloned.1.call-start = ((), (), s32[]{:S(2)}) async-start(), calls=%async_computation.2 | async-start | bytes 3244032 | tf_op jit(solution)/shard_map/all_gather | solution.py:50
  18.3 257.2 %reduce-scatter.5.cloned.1.call-start = ((), (), s32[]{:S(2)}) async-start(), calls=%async_computation.5 | async-start | bytes 3244032 | tf_op jit(solution)/shard_map/reduce_scatter | solution.py:70
  88.5 2.8 copy-start
  91.4 2.3 copy-start.10
  96.4 25.7 %collective-permute-start.4 = (bf16[512,768]{1,0:T(8,128)(2,1)S(1)}, bf16[512,768]{1,0:T(8,128)(2,1)S(1)}, u32[]{:S(2)}, u32[]{:S(2)}) collective-permute-start(bf16[512,768]{1,0:T(8,128)(2,1)S(1)} %get-tuple-element.18), channel_id=1, source_target_pairs={{0,32},{32,0},{1,33},{33,1},{2,34},{34,2},{3,35},{35,3},{4,36},{36... | collective-permute-start | bytes 2359304 | tf_op jit(solution)/shard_map/ppermute | solution.py:11
  122.7 17.3 %collective-permute-start.5 = (bf16[512,768]{1,0:T(8,128)(2,1)S(1)}, bf16[512,768]{1,0:T(8,128)(2,1)S(1)}, u32[]{:S(2)}, u32[]{:S(2)}) collective-permute-start(bf16[512,768]{1,0:T(8,128)(2,1)S(1)} %select_convert_fusion), channel_id=1, source_target_pairs={{0,64},{64,0},{128,192},{192,128},{1,65},{65,1},{129,193},{193,129... | collective-permute-start | bytes 2359304 | tf_op jit(solution)/shard_map/ppermute | solution.py:11
  141.3 2.9 copy-start.4
  146.1 248.6 %reduce-scatter.3.cloned.1.call-start = ((), (), s32[]{:S(2)}) async-start(), calls=%async_computation.3 | async-start | bytes 3244032 | tf_op jit(solution)/shard_map/reduce_scatter | solution.py:70
  156.6 51.0 %slice-start = ((s8[4718592]{0:T(1024)(128)(4,1)}), s8[4194304]{0:T(1024)(128)(4,1)S(1)}, s32[]{:S(2)}) async-start(s8[4718592]{0:T(1024)(128)(4,1)} %bitcast.119), calls=%async_computation.6 | async-start | bytes 8388608
  158.8 6.1 copy-start.1
  158.8 6.1 copy-start.2
  158.8 48.8 %slice-start.1 = ((s8[4718592]{0:T(1024)(128)(4,1)}), s8[524288]{0:T(1024)(128)(4,1)S(1)}, s32[]{:S(2)}) async-start(s8[4718592]{0:T(1024)(128)(4,1)} %bitcast.119), calls=%async_computation.7 | async-start | bytes 1048576
  164.9 22.6 %collective-permute-start.2 = (bf16[512,768]{1,0:T(8,128)(2,1)S(1)}, bf16[512,768]{1,0:T(8,128)(2,1)S(1)}, u32[]{:S(2)}, u32[]{:S(2)}) collective-permute-start(bf16[512,768]{1,0:T(8,128)(2,1)S(1)} %get-tuple-element.16), channel_id=1, source_target_pairs={{0,32},{32,0},{1,33},{33,1},{2,34},{34,2},{3,35},{35,3},{4,36},{36... | collective-permute-start | bytes 2359304 | tf_op jit(solution)/shard_map/ppermute | solution.py:11
  188.2 18.2 %collective-permute-start.3 = (bf16[512,768]{1,0:T(8,128)(2,1)S(1)}, bf16[512,768]{1,0:T(8,128)(2,1)S(1)}, u32[]{:S(2)}, u32[]{:S(2)}) collective-permute-start(bf16[512,768]{1,0:T(8,128)(2,1)S(1)} %select_convert_fusion.1), channel_id=1, source_target_pairs={{0,64},{64,0},{128,192},{192,128},{1,65},{65,1},{129,193},{193,129... | collective-permute-start | bytes 2359304 | tf_op jit(solution)/shard_map/ppermute | solution.py:11
  207.6 2.9 copy-start.5
  212.4 0.9 copy-start.3
  213.3 439.3 %collective-permute-start = (bf16[2,8,6144]{2,1,0:T(8,128)(2,1)S(1)}, bf16[2,8,6144]{2,1,0:T(8,128)(2,1)S(1)}, u32[]{:S(2)}, u32[]{:S(2)}) collective-permute-start(bf16[2,8,6144]{2,1,0:T(8,128)(2,1)S(1)} %bitcast.107), channel_id=1, source_target_pairs={{0,64},{64,0},{128,192},{192,128},{1,65},{65,1},{129,193},{193,129... | collective-permute-start | bytes 589832 | tf_op jit(solution)/shard_map/ppermute | solution.py:11
  395.5 11.3 %collective-permute-start.6 = (bf16[2,8,3072]{2,1,0:T(8,128)(2,1)S(1)}, bf16[2,8,3072]{2,1,0:T(8,128)(2,1)S(1)}, u32[]{:S(2)}, u32[]{:S(2)}) collective-permute-start(bf16[2,8,3072]{2,1,0:T(8,128)(2,1)S(1)} %fusion.64), channel_id=1, source_target_pairs={{0,32},{32,0},{1,33},{33,1},{2,34},{34,2},{3,35},{35,3},{4,36},{36... | collective-permute-start | bytes 294920 | tf_op jit(solution)/shard_map/ppermute | solution.py:11
  397.6 9.2 %copy-start.6 = (bf16[16,3072]{1,0:T(8,128)(2,1)S(1)}, bf16[16,3072]{1,0:T(8,128)(2,1)}, u32[]{:S(2)}) copy-start(bf16[16,3072]{1,0:T(8,128)(2,1)} %reduce-scatter.5.cloned.1.call-done) | copy-start | bytes 294916
  397.6 9.2 %copy-start.7 = (bf16[16,3072]{1,0:T(8,128)(2,1)S(1)}, bf16[16,3072]{1,0:T(8,128)(2,1)}, u32[]{:S(2)}) copy-start(bf16[16,3072]{1,0:T(8,128)(2,1)} %reduce-scatter.3.cloned.1.call-done) | copy-start | bytes 294916
  397.6 9.2 %copy-start.8 = (f32[1,6144]{1,0:T(1,128)S(1)}, f32[1,6144]{1,0:T(1,128)}, u32[]{:S(2)}) copy-start(f32[1,6144]{1,0:T(1,128)} %param.5) | copy-start | bytes 73732
  397.6 9.5 %copy-start.9 = (f32[6144]{0:T(1024)S(1)}, f32[6144]{0:T(1024)}, u32[]{:S(2)}) copy-start(f32[6144]{0:T(1024)} %get-tuple-element.6) | copy-start | bytes 73732
Sparse Core Ops, SparseCore 0:
  17.6 70.8 all-gather.4
  91.0 65.5 all-gather.2
  159.1 116.3 reduce-scatter.4
  278.6 116.0 reduce-scatter.2

commit v2 on v1

v2 whole, which is shorter than its diff:
```python
import functools

import jax
import jax.numpy as jnp
from jax import lax
from jax.experimental import pallas as pl
from jax.experimental.pallas import tpu as pltpu
from jax.sharding import PartitionSpec as P

coeff = 0.7978845608028654
BF = jnp.bfloat16
F32 = jnp.float32
NZ = 8
UP, DOWN = 0, 1


def steps_of(phase, way):
    return 4 if phase == way else 3


def kernel(
    weight_hbm, rows_ref, vec_ref,
    leave_ref, grad_hbm, total_ref,
    w_ref, stage, standard, scale, resid, a_ref,
    part, part_out, part_in, hid_out, hid_in, carried,
    y_own, y_out, y_in, ring_in, wg, tot, back, summed,
    v_out, v_group, v_mid, v_z, v_res, v_all,
    w_sem, wg_sem, group_s, group_r, resid_sem, ag_s, ag_r, sib_s, sib_r,
    dp_s, dp_r, sec_s, sec_r, y_s, y_r, rs_s, rs_r, fin_s, fin_r,
    vg_s, vg_r, vz_s, vz_r, vf_s, vf_r,
):
    sec = lax.axis_index("section")
    rep = lax.axis_index("dp")
    ten = lax.axis_index("tensor")
    core = lax.rem(ten, 2)
    z = lax.rem(lax.div(ten, 2), NZ)
    xlo = lax.div(ten, 2 * NZ)
    x = rep * 2 + xlo
    me = x * 2 + core
    leading = lax.rem(sec, 2) == 0
    model = rows_ref.shape[1]
    quarter = model // 4
    width = w_ref.shape[1]
    partner_sec = sec + 1 - 2 * lax.rem(sec, 2)

    def device(xx, zz, cc):
        return (sec, lax.div(xx, 2), (lax.rem(xx, 2) * NZ + zz) * 2 + cc)

    def member(j):
        return device(lax.div(j, 2), z, lax.rem(j, 2))

    above = device(x, lax.rem(z + 1, NZ), core)
    below = device(x, lax.rem(z + NZ - 1, NZ), core)
    sibling = device(x, z, 1 - core)
    dp_mate = (sec, 1 - rep, ten)
    sec_mate = (partner_sec, rep, ten)

    def copy(src, dst, send, recv, target):
        return pltpu.make_async_remote_copy(
            src_ref=src, dst_ref=dst, send_sem=send, recv_sem=recv,
            device_id=target, device_id_type=pl.DeviceIdType.MESH,
        )

    def zblock(o):
        return lax.rem(z + o, NZ)

    sent = []

    def start(c):
        c.start()
        sent.append(c)

    barrier = pltpu.get_barrier_semaphore()
    friends = [member(lax.rem(me + o, 8)) for o in range(1, 8)]
    friends += [device(x, zblock(o), core) for o in range(1, NZ)]
    friends += [sec_mate]
    for f in friends:
        pl.semaphore_signal(barrier, inc=1, device_id=f, device_id_type=pl.DeviceIdType.MESH)
    w_copy = pltpu.make_async_copy(weight_hbm, w_ref, w_sem)
    w_copy.start()

    @pl.when(leading)
    def _():
        acc = jnp.zeros((16, 1), F32)
        for q in range(4):
            acc += jnp.sum(rows_ref[:, q * quarter:(q + 1) * quarter].astype(F32), axis=1, keepdims=True)
        mean = acc / model
        acc = jnp.zeros((16, 1), F32)
        for q in range(4):
            cen = rows_ref[:, q * quarter:(q + 1) * quarter].astype(F32) - mean
            acc += jnp.sum(cen * cen, axis=1, keepdims=True)
        rs = lax.rsqrt(acc / model + 1e-05)
        scale[...] = jnp.broadcast_to(rs, scale.shape)
        for q in range(4):
            cols = slice(q * quarter, (q + 1) * quarter)
            std = (rows_ref[:, cols].astype(F32) - mean) * rs
            standard[:, cols] = std
            stage[q] = (std * vec_ref[:, cols]).astype(BF)

    @pl.when(jnp.logical_not(leading))
    def _():
        for q in range(4):
            stage[q] = rows_ref[:, q * quarter:(q + 1) * quarter]

    pl.semaphore_wait(barrier, len(friends))

    my_rows = pl.ds(pl.multiple_of(x * 16, 16), 16)
    for o in range(1, 8):
        j = lax.rem(me + o, 8)
        q = lax.div(j, 4) * 2 + lax.rem(j, 2)
        start(copy(
            stage.at[q], a_ref.at[lax.rem(j, 2), core, z, my_rows],
            group_s.at[o], group_r.at[me], member(j),
        ))
    a_ref[core, core, z, my_rows] = stage[rep * 2 + core]
    start(copy(rows_ref, resid, resid_sem.at[0], resid_sem.at[1], sec_mate))

    def group_wait(phase):
        for o in range(4):
            xx = lax.rem(x + o, 4)
            piece = a_ref.at[core, phase, z, pl.ds(pl.multiple_of(xx * 16, 16), 16)]
            sender = xx * 2 + phase

            def wait():
                copy(piece, piece, group_s.at[0], group_r.at[sender], member(sender)).wait_recv()

            if o:
                wait()
            else:
                pl.when(core != phase)(wait)

    def ag_send(phase, way, k):
        o = (NZ - k) % NZ if way == UP else k
        block = a_ref.at[core, phase, zblock(o)]
        start(copy(
            block, block, ag_s.at[phase, way, k], ag_r.at[phase, way, k],
            above if way == UP else below,
        ))

    def ag_wait(phase, way, k):
        o = NZ - 1 - k if way == UP else k + 1
        block = a_ref.at[core, phase, zblock(o)]
        copy(
            block, block, ag_s.at[phase, way, k], ag_r.at[phase, way, k],
            above if way == UP else below,
        ).wait_recv()
        return o

    def sib_send(phase, o):
        block = a_ref.at[core, phase, zblock(o)]
        start(copy(block, block, sib_s.at[phase, o], sib_r.at[phase, o], sibling))

    def sib_wait(phase, o):
        block = a_ref.at[1 - core, phase, zblock(o)]
        copy(block, block, sib_s.at[phase, o], sib_r.at[phase, o], sibling).wait_recv()

    def forward(phase, j):
        for way in (UP, DOWN):
            count = steps_of(phase, way)
            if j > count:
                continue
            o = ag_wait(phase, way, j - 1)
            if j < count:
                ag_send(phase, way, j)
            sib_send(phase, o)

    def pair(k):
        return (NZ - k, k) if k < 4 else (4, 0)

    def mm1(phase, k):
        u = phase * 4 + k - 1
        o1, o2 = pair(k)
        sib_wait(phase, o1)
        sib_wait(phase, o2)
        b1, b2 = zblock(o1), zblock(o2)

        @pl.loop(0, width // 256)
        def _(n):
            cols = pl.ds(pl.multiple_of(n * 256, 256), 256)
            acc = None
            for q in range(2):
                left = jnp.concatenate([a_ref[q, phase, b1], a_ref[q, phase, b2]], axis=0)
                d = jnp.dot(left, w_ref[q * quarter:(q + 1) * quarter, cols], preferred_element_type=F32)
                acc = d if acc is None else acc + d
            part[u, :, cols] = acc
            part_out[u, :, cols] = acc.astype(BF)

        start(copy(part_out.at[u], part_in.at[u], dp_s.at[u], dp_r.at[u], dp_mate))

    def mid1(phase, k):
        u = phase * 4 + k - 1
        copy(part_out.at[u], part_in.at[u], dp_s.at[u], dp_r.at[u], dp_mate).wait_recv()

        @pl.when(leading)
        def _():
            @pl.loop(0, 8)
            def _(n):
                rows = pl.ds(pl.multiple_of(n * 16, 16), 16)
                p = part[u, rows, :] + part_in[u, rows, :].astype(F32)
                sq = p * p
                inner = jnp.tanh(coeff * (p + 0.044715 * sq * p))
                one = 1.0 + inner
                hid_out[u, rows, :] = (0.5 * p * one).astype(BF)
                part[u, rows, :] = 0.5 * one + 0.5 * p * (1.0 - inner * inner) * coeff * (
                    1.0 + 3.0 * 0.044715 * sq
                )

        @pl.when(jnp.logical_not(leading))
        def _():
            @pl.loop(0, 8)
            def _(n):
                rows = pl.ds(pl.multiple_of(n * 16, 16), 16)
                hid_out[u, rows, :] = (part[u, rows, :] + part_in[u, rows, :].astype(F32)).astype(BF)

        start(copy(hid_out.at[u], hid_in.at[u], sec_s.at[u], sec_r.at[u], sec_mate))

    def mid2(phase, k):
        u = phase * 4 + k - 1
        copy(hid_out.at[u], hid_in.at[u], sec_s.at[u], sec_r.at[u], sec_mate).wait_recv()
        for i, o in enumerate(pair(k)):
            b = zblock(o)

            @pl.when(leading)
            def _():
                @pl.loop(0, 4)
                def _(n):
                    src = pl.ds(pl.multiple_of(i * 64 + n * 16, 16), 16)
                    dst = pl.ds(pl.multiple_of(n * 16, 16), 16)
                    carried[phase, b, dst, :] = (hid_in[u, src, :].astype(F32) * part[u, src, :]).astype(BF)

            @pl.when(jnp.logical_not(leading))
            def _():
                carried[phase, b] = hid_in[u, i * 64:(i + 1) * 64, :]

    def mm2(phase, k):
        o1, o2 = pair(k)
        b1, b2 = zblock(o1), zblock(o2)
        for half, dst in ((1 - core, y_out), (core, y_own)):
            @pl.loop(0, quarter // 256)
            def _(n):
                left = jnp.concatenate([carried[phase, b1], carried[phase, b2]], axis=0)
                right = w_ref[pl.ds(pl.multiple_of(half * quarter + n * 256, 256), 256), :]
                d = lax.dot_general(
                    left, right, (((1,), (1,)), ((), ())), preferred_element_type=F32
                ).astype(BF)
                cols = pl.ds(pl.multiple_of(n * 256, 256), 256)
                dst[phase, o1, :, cols] = d[:64]
                dst[phase, o2, :, cols] = d[64:]

            if dst is y_out:
                for o in (o1, o2):
                    start(copy(
                        y_out.at[phase, o], y_in.at[phase, o], y_s.at[phase, o], y_r.at[phase, o], sibling
                    ))

    def y_wait(phase, o):
        copy(
            y_out.at[phase, o], y_in.at[phase, o], y_s.at[phase, o], y_r.at[phase, o], sibling
        ).wait_recv()

    def rs_copy(phase, way, i):
        count = steps_of(phase, way)
        o = count - i if way == UP else NZ - (count - i)
        return o, copy(
            y_own.at[phase, o], ring_in.at[phase, way, i], rs_s.at[phase, way, i], rs_r.at[phase, way, i],
            above if way == UP else below,
        )

    def rs_step(phase, way, i):
        o, c = rs_copy(phase, way, i)
        y_wait(phase, o)
        if i:
            rs_copy(phase, way, i - 1)[1].wait_recv()

        @pl.loop(0, 4)
        def _(n):
            rows = pl.ds(pl.multiple_of(n * 16, 16), 16)
            s = y_own[phase, o, rows, :].astype(F32) + y_in[phase, o, rows, :].astype(F32)
            if i:
                s += ring_in[phase, way, i - 1, rows, :].astype(F32)
            y_own[phase, o, rows, :] = s.astype(BF)

        start(c)

    def rs_final(phase):
        y_wait(phase, 0)
        last = [steps_of(phase, way) - 1 for way in (UP, DOWN)]
        for way in (UP, DOWN):
            rs_copy(phase, way, last[way])[1].wait_recv()

        @pl.loop(0, 4)
        def _(n):
            rows = pl.ds(pl.multiple_of(n * 16, 16), 16)
            s = y_own[phase, 0, rows, :].astype(F32) + y_in[phase, 0, rows, :].astype(F32)
            for way in (UP, DOWN):
                s += ring_in[phase, way, last[way], rows, :].astype(F32)
            tot[phase, rows, :] = s.astype(BF)

        for o in range(4):
            xx = lax.rem(x + o, 4)
            piece = tot.at[phase, pl.ds(pl.multiple_of(xx * 16, 16), 16)]
            c = copy(
                piece, back.at[me], fin_s.at[phase, o], fin_r.at[me], device(xx, z, phase)
            )
            if o:
                start(c)
            else:
                @pl.when(core != phase)
                def _():
                    c.start()

                @pl.when(core == phase)
                def _():
                    back[me] = tot[phase, my_rows, :]

    def wgrad(first, count):
        @pl.loop(first, first + count)
        def _(t):
            q = lax.div(t, quarter // 256)
            cols = pl.ds(pl.multiple_of(lax.rem(t, quarter // 256) * 256, 256), 256)
            left = a_ref[q, :, :, :, cols].reshape(-1, 256)
            right = carried[...].reshape(-1, width)
            d = lax.dot_general(left, right, (((0,), (0,)), ((), ())), preferred_element_type=F32)
            wg[pl.ds(pl.multiple_of(t * 256, 256), 256), :] = d.astype(BF)

    for phase in (0, 1):
        group_wait(phase)
        ag_send(phase, UP, 0)
        ag_send(phase, DOWN, 0)
        sib_send(phase, 0)
    w_copy.wait()
    for j in range(1, 5):
        for phase in (0, 1):
            forward(phase, j)
            mm1(phase, j)
        if j >= 3:
            for phase in (0, 1):
                mid2(phase, j - 2)
                mm2(phase, j - 2)
        if j >= 2:
            for phase in (0, 1):
                mid1(phase, j - 1)
    for phase in (0, 1):
        mid1(phase, 4)
    for phase in (0, 1):
        mid2(phase, 3)
        mm2(phase, 3)
    for phase in (0, 1):
        mid2(phase, 4)
        mm2(phase, 4)
        rs_step(phase, UP, 0)
        rs_step(phase, DOWN, 0)
    tiles = model // 512
    per = tiles // 4
    copies = []
    for i in range(1, 5):
        wgrad((i - 1) * per, per)
        rows = pl.ds((i - 1) * per * 256, per * 256)
        c = pltpu.make_async_copy(wg.at[rows], grad_hbm.at[rows], wg_sem.at[i - 1])
        c.start()
        copies.append(c)
        for phase in (0, 1):
            for way in (UP, DOWN):
                if i < steps_of(phase, way):
                    rs_step(phase, way, i)
    for phase in (0, 1):
        rs_final(phase)

    copy(rows_ref, resid, resid_sem.at[0], resid_sem.at[1], sec_mate).wait_recv()
    for o in range(1, 8):
        j = lax.rem(me + o, 8)
        copy(back.at[j], back.at[j], fin_s.at[0, 0], fin_r.at[j], member(j)).wait_recv()

    def quarter_sum(q):
        j = (q // 2) * 4 + q % 2
        return back[j].astype(F32) + back[j + 2].astype(F32)

    chunk = model // 8

    @pl.when(leading)
    def _():
        mean = jnp.zeros((16, 1), F32)
        mix = jnp.zeros((16, 1), F32)
        for q in range(4):
            cols = slice(q * quarter, (q + 1) * quarter)
            s = quarter_sum(q)
            std = standard[:, cols]
            v = jnp.sum(s * std, axis=0, keepdims=True)
            v_out[2 * q] = v[:, :chunk]
            v_out[2 * q + 1] = v[:, chunk:]
            g = s * vec_ref[:, cols]
            summed[:, cols] = g
            mean += jnp.sum(g, axis=1, keepdims=True)
            mix += jnp.sum(g * std, axis=1, keepdims=True)
        mean = mean / model
        mix = mix / model
        rs = scale[:, 0:1]
        for q in range(4):
            cols = slice(q * quarter, (q + 1) * quarter)
            through = (summed[:, cols] - mean - standard[:, cols] * mix) * rs
            leave_ref[:, cols] = (resid[:, cols].astype(F32) + through).astype(BF)

    @pl.when(jnp.logical_not(leading))
    def _():
        for q in range(4):
            cols = slice(q * quarter, (q + 1) * quarter)
            v = jnp.sum(rows_ref[:, cols].astype(F32), axis=0, keepdims=True)
            v_out[2 * q] = v[:, :chunk]
            v_out[2 * q + 1] = v[:, chunk:]
            leave_ref[:, cols] = (resid[:, cols].astype(F32) + quarter_sum(q) + vec_ref[:, cols]).astype(BF)

    for o in range(1, 8):
        j = lax.rem(me + o, 8)
        start(copy(v_out.at[j], v_group.at[me], vg_s.at[o], vg_r.at[me], member(j)))
    v_group[me] = v_out[me]
    for o in range(1, 8):
        j = lax.rem(me + o, 8)
        copy(v_group.at[j], v_group.at[j], vg_s.at[0], vg_r.at[j], member(j)).wait_recv()
    v_mid[...] = jnp.sum(v_group[...], axis=0)
    for o in range(1, NZ):
        start(copy(v_mid, v_z.at[z], vz_s.at[o], vz_r.at[z], device(x, zblock(o), core)))
    v_z[z] = v_mid[...]
    for o in range(1, NZ):
        b = zblock(o)
        copy(v_z.at[b], v_z.at[b], vz_s.at[0], vz_r.at[b], device(x, b, core)).wait_recv()
    v_res[...] = jnp.sum(v_z[...], axis=0)
    for o in range(1, 8):
        j = lax.rem(me + o, 8)
        start(copy(v_res, v_all.at[me], vf_s.at[o], vf_r.at[me], member(j)))
    v_all[me] = v_res[...]
    for o in range(1, 8):
        j = lax.rem(me + o, 8)
        copy(v_all.at[j], v_all.at[j], vf_s.at[0], vf_r.at[j], member(j)).wait_recv()
    for j in range(8):
        total_ref[:, j * chunk:(j + 1) * chunk] = v_all[j]

    for c in sent:
        c.wait_send()
    for phase in (0, 1):
        @pl.when(core != phase)
        def _():
            copy(
                tot.at[phase, my_rows], back.at[me], fin_s.at[phase, 0], fin_r.at[me], device(x, z, phase)
            ).wait_send()
    for c in copies:
        c.wait()


def local(weights, arriving, vectors):
    _, half, width = weights.shape
    _, micro, rows, model = arriving.shape
    quarter = model // 4
    chunk = model // 8
    dma = pltpu.SemaphoreType.DMA
    vm = pltpu.VMEM
    block = (64, quarter)
    leaving, weight_grad, totals = pl.pallas_call(
        kernel,
        out_shape=(
            jax.ShapeDtypeStruct((micro * rows, model), BF),
            jax.ShapeDtypeStruct((half, width), BF),
            jax.ShapeDtypeStruct((1, model), F32),
        ),
        in_specs=[
            pl.BlockSpec(memory_space=pl.ANY),
            pl.BlockSpec(memory_space=pltpu.VMEM),
            pl.BlockSpec(memory_space=pltpu.VMEM),
        ],
        out_specs=(
            pl.BlockSpec(memory_space=pltpu.VMEM),
            pl.BlockSpec(memory_space=pl.ANY),
            pl.BlockSpec(memory_space=pltpu.VMEM),
        ),
        scratch_shapes=[
            vm((half, width), BF),
            vm((4, 16, quarter), BF),
            vm((16, model), F32),
            vm((16, 128), F32),
            vm((16, model), BF),
            vm((2, 2, NZ, *block), BF),
            vm((8, 128, width), F32),
            vm((8, 128, width), BF),
            vm((8, 128, width), BF),
            vm((8, 128, width), BF),
            vm((8, 128, width), BF),
            vm((2, NZ, 64, width), BF),
            vm((2, NZ, *block), BF),
            vm((2, NZ, *block), BF),
            vm((2, NZ, *block), BF),
            vm((2, 2, 4, *block), BF),
            vm((half, width), BF),
            vm((2, *block), BF),
            vm((8, 16, quarter), BF),
            vm((16, model), F32),
            vm((8, 1, chunk), F32),
            vm((8, 1, chunk), F32),
            vm((1, chunk), F32),
            vm((NZ, 1, chunk), F32),
            vm((1, chunk), F32),
            vm((8, 1, chunk), F32),
            dma, dma((4,)), dma((8,)), dma((8,)), dma((2,)),
            dma((2, 2, 4)), dma((2, 2, 4)), dma((2, NZ)), dma((2, NZ)),
            dma((8,)), dma((8,)), dma((8,)), dma((8,)),
            dma((2, NZ)), dma((2, NZ)), dma((2, 2, 4)), dma((2, 2, 4)),
            dma((2, 4)), dma((8,)),
            dma((8,)), dma((8,)), dma((8,)), dma((8,)), dma((8,)), dma((8,)),
        ],
        compiler_params=pltpu.CompilerParams(
            collective_id=0, has_side_effects=True, vmem_limit_bytes=56 * 1024 * 1024
        ),
        cost_estimate=pl.CostEstimate(
            flops=3 * 2 * 1024 * half * width, bytes_accessed=4 * half * width, transcendentals=1024 * width
        ),
    )(weights[0], arriving[0].reshape(micro * rows, model), vectors)
    return (leaving.reshape(1, micro, rows, model), weight_grad[None], totals)


def solution(mesh):
    placed = (
        P("section", "dp", "tensor"),
        P("section", None, ("dp", "tensor"), None),
        P("section", None),
    )
    return jax.shard_map(
        local,
        mesh=mesh,
        in_specs=placed,
        out_specs=(
            P("section", None, ("dp", "tensor"), None),
            P("section", "dp", "tensor"),
            P("section", None),
        ),
        check_vma=False,
    )
```

time: 664 us -> 147 us (0.22)
  waiting for transfers between devices: 334 us -> 0 us
  blocking collectives: 245 us -> 0 us
  Pallas kernels: 0 us -> 139 us
  matrix products: 23.6 us -> 0 us
  other arithmetic: 20 us -> 0 us
  starting transfers between devices: 15.1 us -> 0 us
  between operations: 14 us -> 0.64 us
    psum x1 -> x0, blocking collectives: 245 us -> none  [local(): totals = lax.psum(vector_term, ('dp', 'tensor'))]
    reduce_scatter x2 -> x0, waiting for transfers between devices: 176 us -> none  [local(): total = lax.psum_scatter(product, 'tensor', scatter_dimension=0, tiled=True)]
    pallas_call x0 -> x1, Pallas kernels: none -> 139 us  [local(): pl.pallas_call(kernel, out_shape=(jax.ShapeDtypeStruct((micro * rows, mod...]
    all_gather x2 -> x0, waiting for transfers between devices: 80.7 us -> none  [local(): gathered = lax.all_gather(pair, 'tensor', axis=0, tiled=True)]
    ppermute x7 -> x0, waiting for transfers between devices: 77.8 us -> none  [swap(): return lax.ppermute(block, axis, [(i, i ^ 1) for i in range(count)])]
    dot_general x5 -> x0, matrix products: 23.6 us -> none  [the longest x1 9.15 us: local(): lax.dot_general(jnp.concatenate(gathers, axis=0), jnp.concatenate(carries...]
    ppermute x7 -> x0, starting transfers between devices: 14.9 us -> none  [swap(): return lax.ppermute(block, axis, [(i, i ^ 1) for i in range(count)])]
    select_n x8 -> x0, other arithmetic: 8.18 us -> none  [the longest x2 2.45 us: local(): jnp.where(leading, (back_hidden.astype(jnp.float32) * gelu_slope(preact))...]
  transfers between devices with their start and end apart: 11 -> 0, of which waited for: 9 -> 0; matrix products, arithmetic and copies ran while one was open for 6% -> 0% of each run, Pallas kernels for 0% -> 0%
where the time goes in v2:
time: 147 us
  Pallas kernels  139 us (95%)
  local copies, waits for them, and re-layouts  7.06 us (5%)
    pallas_call x1, Pallas kernels, local(): pl.pallas_call(kernel, out_shape=(jax.ShapeDtypeStruct((micro * rows, mod...  139 us
    unnamed x5, local copies, waits for them, and re-layouts  7.06 us

profile of v2, /device:TPU:1, one launch (start us, length us, event | category | flops | bytes accessed | tf_op | source)
XLA Modules:
  0.0 146.9 jit_solution(8196579298365312336)
XLA Ops:
  0.6 139.2 %shard_map.58 = (bf16[16,6144]{1,0:T(8,128)(2,1)}, bf16[3072,768]{1,0:T(8,128)(2,1)}, f32[1,6144]{1,0:T(1,128)}) custom-call(bf16[3072,768]{1,0:T(8,128)(2,1)} %bitcast.6, bf16[16,6144]{1,0:T(8,128)(2,1)} %bitcast.7, f32[1,6144]{1,0:T(1,128)} %vec_ref.1), custom_call_target="tpu_custom_call" | custom-call | flops 14495514624 | bytes 9437184 | tf_op jit(solution)/shard_map/pallas_call | solution.py:457
  139.8 1.6 %copy.9 = bf16[1,2,8,6144]{3,2,1,0:T(8,128)(2,1)} copy(bf16[1,2,8,6144]{3,2,1,0:T(8,128)(2,1)} %bitcast.5) | data formatting | bytes 393216
  141.4 0.0 copy-start
  141.4 4.8 %copy.10 = bf16[1,3072,768]{2,1,0:T(8,128)(2,1)} copy(bf16[1,3072,768]{2,1,0:T(8,128)(2,1)} %bitcast.4) | data formatting | bytes 9437184
  146.3 0.0 copy-done
  146.3 0.6 copy.11
Async XLA Ops:
  141.4 4.8 %copy-start = (f32[1,6144]{1,0:T(1,128)S(1)}, f32[1,6144]{1,0:T(1,128)}, u32[]{:S(2)}) copy-start(f32[1,6144]{1,0:T(1,128)} %get-tuple-element.14) | copy-start | bytes 73732

commit v3 on v2

--- a/solution.py
+++ b/solution.py
@@ -24,10 +24,10 @@
     w_ref, stage, standard, scale, resid, a_ref,
     part, part_out, part_in, hid_out, hid_in, carried,
     y_own, y_out, y_in, ring_in, wg, tot, back, summed,
-    v_out, v_group, v_mid, v_z, v_res, v_all,
+    v_out, v_in,
     w_sem, wg_sem, group_s, group_r, resid_sem, ag_s, ag_r, sib_s, sib_r,
     dp_s, dp_r, sec_s, sec_r, y_s, y_r, rs_s, rs_r, fin_s, fin_r,
-    vg_s, vg_r, vz_s, vz_r, vf_s, vf_r,
+    v_s, v_r,
 ):
     sec = lax.axis_index("section")
     rep = lax.axis_index("dp")
@@ -72,8 +72,12 @@
 
     barrier = pltpu.get_barrier_semaphore()
     friends = [member(lax.rem(me + o, 8)) for o in range(1, 8)]
-    friends += [device(x, zblock(o), core) for o in range(1, NZ)]
-    friends += [sec_mate]
+    z2 = z + 2 - 4 * lax.rem(lax.div(z, 2), 2)
+    doubling = [
+        sibling, device(rep * 2 + 1 - xlo, z, core), device(x, z + 1 - 2 * lax.rem(z, 2), core),
+        device(x, z2, core), device(x, zblock(4), core), dp_mate,
+    ]
+    friends += [above, below, doubling[3], doubling[4], sec_mate]
     for f in friends:
         pl.semaphore_signal(barrier, inc=1, device_id=f, device_id_type=pl.DeviceIdType.MESH)
     w_copy = pltpu.make_async_copy(weight_hbm, w_ref, w_sem)
@@ -164,22 +168,22 @@
                 ag_send(phase, way, j)
             sib_send(phase, o)
 
-    def pair(k):
-        return (NZ - k, k) if k < 4 else (4, 0)
-
-    def mm1(phase, k):
-        u = phase * 4 + k - 1
-        o1, o2 = pair(k)
-        sib_wait(phase, o1)
-        sib_wait(phase, o2)
-        b1, b2 = zblock(o1), zblock(o2)
+    units = [((0, 0), (1, 0))]
+    for k in (1, 2, 3):
+        units += [((phase, NZ - k), (phase, k)) for phase in (0, 1)]
+    units += [((0, 4), (1, 4))]
+
+    def mm1(u):
+        for phase, o in units[u]:
+            sib_wait(phase, o)
+        (p1, b1), (p2, b2) = [(phase, zblock(o)) for phase, o in units[u]]
 
         @pl.loop(0, width // 256)
         def _(n):
             cols = pl.ds(pl.multiple_of(n * 256, 256), 256)
             acc = None
             for q in range(2):
-                left = jnp.concatenate([a_ref[q, phase, b1], a_ref[q, phase, b2]], axis=0)
+                left = jnp.concatenate([a_ref[q, p1, b1], a_ref[q, p2, b2]], axis=0)
                 d = jnp.dot(left, w_ref[q * quarter:(q + 1) * quarter, cols], preferred_element_type=F32)
                 acc = d if acc is None else acc + d
             part[u, :, cols] = acc
@@ -187,8 +191,7 @@
 
         start(copy(part_out.at[u], part_in.at[u], dp_s.at[u], dp_r.at[u], dp_mate))
 
-    def mid1(phase, k):
-        u = phase * 4 + k - 1
+    def mid1(u):
         copy(part_out.at[u], part_in.at[u], dp_s.at[u], dp_r.at[u], dp_mate).wait_recv()
 
         @pl.when(leading)
@@ -214,10 +217,9 @@
 
         start(copy(hid_out.at[u], hid_in.at[u], sec_s.at[u], sec_r.at[u], sec_mate))
 
-    def mid2(phase, k):
-        u = phase * 4 + k - 1
+    def mid2(u):
         copy(hid_out.at[u], hid_in.at[u], sec_s.at[u], sec_r.at[u], sec_mate).wait_recv()
-        for i, o in enumerate(pair(k)):
+        for i, (phase, o) in enumerate(units[u]):
             b = zblock(o)
 
             @pl.when(leading)
@@ -232,23 +234,23 @@
             def _():
                 carried[phase, b] = hid_in[u, i * 64:(i + 1) * 64, :]
 
-    def mm2(phase, k):
-        o1, o2 = pair(k)
+    def mm2(u):
+        (p1, o1), (p2, o2) = units[u]
         b1, b2 = zblock(o1), zblock(o2)
         for half, dst in ((1 - core, y_out), (core, y_own)):
             @pl.loop(0, quarter // 256)
             def _(n):
-                left = jnp.concatenate([carried[phase, b1], carried[phase, b2]], axis=0)
+                left = jnp.concatenate([carried[p1, b1], carried[p2, b2]], axis=0)
                 right = w_ref[pl.ds(pl.multiple_of(half * quarter + n * 256, 256), 256), :]
                 d = lax.dot_general(
                     left, right, (((1,), (1,)), ((), ())), preferred_element_type=F32
                 ).astype(BF)
                 cols = pl.ds(pl.multiple_of(n * 256, 256), 256)
-                dst[phase, o1, :, cols] = d[:64]
-                dst[phase, o2, :, cols] = d[64:]
+                dst[p1, o1, :, cols] = d[:64]
+                dst[p2, o2, :, cols] = d[64:]
 
             if dst is y_out:
-                for o in (o1, o2):
+                for phase, o in units[u]:
                     start(copy(
                         y_out.at[phase, o], y_in.at[phase, o], y_s.at[phase, o], y_r.at[phase, o], sibling
                     ))
@@ -321,7 +323,34 @@
             left = a_ref[q, :, :, :, cols].reshape(-1, 256)
             right = carried[...].reshape(-1, width)
             d = lax.dot_general(left, right, (((0,), (0,)), ((), ())), preferred_element_type=F32)
-            wg[pl.ds(pl.multiple_of(t * 256, 256), 256), :] = d.astype(BF)
+            rows = pl.ds(pl.multiple_of(t * 256, 256), 256)
+            wg[rows, :] = d.astype(BF)
+
+            @pl.when(leading)
+            def _():
+                fold = jnp.zeros((256, 128), F32)
+                for m in range(width // 128):
+                    lanes = slice(m * 128, (m + 1) * 128)
+                    fold += d[:, lanes] * w_ref[rows, lanes].astype(F32)
+                line = jnp.sum(fold.T, axis=0, keepdims=True)
+                gains = vec_ref[:, pl.ds(pl.multiple_of(rep * half_model + t * 256, 256), 256)]
+                v_out[0, :, rows] = line / gains
+
+        rows = pl.ds(first * 256, count * 256)
+        c = pltpu.make_async_copy(wg.at[rows], grad_hbm.at[rows], wg_sem.at[len(copies)])
+        c.start()
+        copies.append(c)
+
+    def vec_copy(t):
+        return copy(v_out.at[t], v_in.at[t], v_s.at[t], v_r.at[t], doubling[t])
+
+    def vec_next(t):
+        vec_copy(t).wait_recv()
+        v_out[t + 1] = v_out[t] + v_in[t]
+        start(vec_copy(t + 1))
+
+    half_model = model // 2
+    copies = []
 
     for phase in (0, 1):
         group_wait(phase)
@@ -329,42 +358,60 @@
         ag_send(phase, DOWN, 0)
         sib_send(phase, 0)
     w_copy.wait()
-    for j in range(1, 5):
-        for phase in (0, 1):
-            forward(phase, j)
-            mm1(phase, j)
-        if j >= 3:
-            for phase in (0, 1):
-                mid2(phase, j - 2)
-                mm2(phase, j - 2)
-        if j >= 2:
-            for phase in (0, 1):
-                mid1(phase, j - 1)
-    for phase in (0, 1):
-        mid1(phase, 4)
-    for phase in (0, 1):
-        mid2(phase, 3)
-        mm2(phase, 3)
-    for phase in (0, 1):
-        mid2(phase, 4)
-        mm2(phase, 4)
-        rs_step(phase, UP, 0)
-        rs_step(phase, DOWN, 0)
-    tiles = model // 512
-    per = tiles // 4
-    copies = []
-    for i in range(1, 5):
+    mm1(0)
+    for u in range(1, 8):
+        if u < 7:
+            forward((u - 1) % 2, (u + 1) // 2)
+        else:
+            forward(0, 4)
+            forward(1, 4)
+        mm1(u)
+        if u >= 2:
+            mid1(u - 2)
+        if u >= 4:
+            mid2(u - 4)
+        if u >= 5:
+            mm2(u - 5)
+    mid2(4)
+    mid1(6)
+    mid2(5)
+    mm2(5)
+    rs_step(0, DOWN, 0)
+    mid1(7)
+    mid2(6)
+    mm2(6)
+    rs_step(1, UP, 0)
+    mm2(3)
+    rs_step(0, DOWN, 1)
+    mid2(7)
+    mm2(7)
+    rs_step(0, UP, 0)
+    rs_step(1, DOWN, 0)
+    mm2(4)
+    rs_step(1, UP, 1)
+    rs_step(0, DOWN, 2)
+    rs_step(1, UP, 2)
+    per = model // 512 // 3
+    for i in range(1, 4):
         wgrad((i - 1) * per, per)
-        rows = pl.ds((i - 1) * per * 256, per * 256)
-        c = pltpu.make_async_copy(wg.at[rows], grad_hbm.at[rows], wg_sem.at[i - 1])
-        c.start()
-        copies.append(c)
-        for phase in (0, 1):
-            for way in (UP, DOWN):
-                if i < steps_of(phase, way):
-                    rs_step(phase, way, i)
-    for phase in (0, 1):
-        rs_final(phase)
+        rs_step(0, UP, i)
+        rs_step(1, DOWN, i)
+
+    @pl.when(jnp.logical_not(leading))
+    def _():
+        for q in range(2):
+            line = jnp.zeros((1, quarter), F32)
+            for xx in (xlo, xlo + 2):
+                rows = pl.ds(pl.multiple_of(xx * 16, 16), 16)
+                line += jnp.sum(a_ref[q, core, z, rows].astype(F32), axis=0, keepdims=True)
+            v_out[0, :, q * quarter:(q + 1) * quarter] = line
+
+    start(vec_copy(0))
+    vec_next(0)
+    rs_final(0)
+    rs_final(1)
+    vec_next(1)
+    vec_next(2)
 
     copy(rows_ref, resid, resid_sem.at[0], resid_sem.at[1], sec_mate).wait_recv()
     for o in range(1, 8):
@@ -375,8 +422,6 @@
         j = (q // 2) * 4 + q % 2
         return back[j].astype(F32) + back[j + 2].astype(F32)
 
-    chunk = model // 8
-
     @pl.when(leading)
     def _():
         mean = jnp.zeros((16, 1), F32)
@@ -385,9 +430,6 @@
             cols = slice(q * quarter, (q + 1) * quarter)
             s = quarter_sum(q)
             std = standard[:, cols]
-            v = jnp.sum(s * std, axis=0, keepdims=True)
-            v_out[2 * q] = v[:, :chunk]
-            v_out[2 * q + 1] = v[:, chunk:]
             g = s * vec_ref[:, cols]
             summed[:, cols] = g
             mean += jnp.sum(g, axis=1, keepdims=True)
@@ -404,35 +446,15 @@
     def _():
         for q in range(4):
             cols = slice(q * quarter, (q + 1) * quarter)
-            v = jnp.sum(rows_ref[:, cols].astype(F32), axis=0, keepdims=True)
-            v_out[2 * q] = v[:, :chunk]
-            v_out[2 * q + 1] = v[:, chunk:]
             leave_ref[:, cols] = (resid[:, cols].astype(F32) + quarter_sum(q) + vec_ref[:, cols]).astype(BF)
 
-    for o in range(1, 8):
-        j = lax.rem(me + o, 8)
-        start(copy(v_out.at[j], v_group.at[me], vg_s.at[o], vg_r.at[me], member(j)))
-    v_group[me] = v_out[me]
-    for o in range(1, 8):
-        j = lax.rem(me + o, 8)
-        copy(v_group.at[j], v_group.at[j], vg_s.at[0], vg_r.at[j], member(j)).wait_recv()
-    v_mid[...] = jnp.sum(v_group[...], axis=0)
-    for o in range(1, NZ):
-        start(copy(v_mid, v_z.at[z], vz_s.at[o], vz_r.at[z], device(x, zblock(o), core)))
-    v_z[z] = v_mid[...]
-    for o in range(1, NZ):
-        b = zblock(o)
-        copy(v_z.at[b], v_z.at[b], vz_s.at[0], vz_r.at[b], device(x, b, core)).wait_recv()
-    v_res[...] = jnp.sum(v_z[...], axis=0)
-    for o in range(1, 8):
-        j = lax.rem(me + o, 8)
-        start(copy(v_res, v_all.at[me], vf_s.at[o], vf_r.at[me], member(j)))
-    v_all[me] = v_res[...]
-    for o in range(1, 8):
-        j = lax.rem(me + o, 8)
-        copy(v_all.at[j], v_all.at[j], vf_s.at[0], vf_r.at[j], member(j)).wait_recv()
-    for j in range(8):
-        total_ref[:, j * chunk:(j + 1) * chunk] = v_all[j]
+    vec_next(3)
+    vec_next(4)
+    vec_copy(5).wait_recv()
+    mine = pl.ds(pl.multiple_of(rep * half_model, 128), half_model)
+    other = pl.ds(pl.multiple_of((1 - rep) * half_model, 128), half_model)
+    total_ref[:, mine] = v_out[5]
+    total_ref[:, other] = v_in[5]
 
     for c in sent:
         c.wait_send()
@@ -450,7 +472,6 @@
     _, half, width = weights.shape
     _, micro, rows, model = arriving.shape
     quarter = model // 4
-    chunk = model // 8
     dma = pltpu.SemaphoreType.DMA
     vm = pltpu.VMEM
     block = (64, quarter)
@@ -492,21 +513,17 @@
             vm((2, *block), BF),
             vm((8, 16, quarter), BF),
             vm((16, model), F32),
-            vm((8, 1, chunk), F32),
-            vm((8, 1, chunk), F32),
-            vm((1, chunk), F32),
-            vm((NZ, 1, chunk), F32),
-            vm((1, chunk), F32),
-            vm((8, 1, chunk), F32),
+            vm((6, 1, half), F32),
+            vm((6, 1, half), F32),
             dma, dma((4,)), dma((8,)), dma((8,)), dma((2,)),
             dma((2, 2, 4)), dma((2, 2, 4)), dma((2, NZ)), dma((2, NZ)),
             dma((8,)), dma((8,)), dma((8,)), dma((8,)),
             dma((2, NZ)), dma((2, NZ)), dma((2, 2, 4)), dma((2, 2, 4)),
             dma((2, 4)), dma((8,)),
-            dma((8,)), dma((8,)), dma((8,)), dma((8,)), dma((8,)), dma((8,)),
+            dma((6,)), dma((6,)),
         ],
         compiler_params=pltpu.CompilerParams(
-            collective_id=0, has_side_effects=True, vmem_limit_bytes=56 * 1024 * 1024
+            collective_id=0, has_side_effects=True, vmem_limit_bytes=46 * 1024 * 1024
         ),
         cost_estimate=pl.CostEstimate(
             flops=3 * 2 * 1024 * half * width, bytes_accessed=4 * half * width, transcendentals=1024 * width

time: 147 us -> 129 us (0.88); the launches traced: 147 us -> 127 us
  Pallas kernels: 139 us -> 122 us
  local copies, waits for them, and re-layouts: 7.06 us -> 5.13 us
    pallas_call x1, Pallas kernels: 139 us -> 122 us  [local(): pl.pallas_call(kernel, out_shape=(jax.ShapeDtypeStruct((micro * rows, mod...]
    unnamed x5 -> x7, local copies, waits for them, and re-layouts: 7.06 us -> 5.13 us
where the time goes in v3:
time: 129 us; the launch traced here: 127 us
  Pallas kernels  122 us (95%)
  local copies, waits for them, and re-layouts  5.13 us (4%)
    pallas_call x1, Pallas kernels, local(): pl.pallas_call(kernel, out_shape=(jax.ShapeDtypeStruct((micro * rows, mod...  122 us
    unnamed x7, local copies, waits for them, and re-layouts  5.13 us

profile of v3, /device:TPU:1, one launch (start us, length us, event | category | flops | bytes accessed | tf_op | source)
XLA Modules:
  0.0 127.3 jit_solution(12400029764986555090)
XLA Ops:
  0.6 0.0 copy-start
  0.6 0.9 copy-done
  1.6 0.0 copy-start.1
  1.6 0.7 copy-done.1
  2.3 121.5 %shard_map.58 = (bf16[16,6144]{1,0:T(8,128)(2,1)S(1)}, bf16[3072,768]{1,0:T(8,128)(2,1)S(1)}, f32[1,6144]{1,0:T(1,128)S(1)}) custom-call(bf16[3072,768]{1,0:T(8,128)(2,1)} %bitcast.7, bf16[16,6144]{1,0:T(8,128)(2,1)S(1)} %bitcast.6, f32[1,6144]{1,0:T(1,128)S(1)} %copy-done.1), custom_call_target="tpu_custom_call" | custom-call | flops 14495514624 | bytes 9437184 | tf_op jit(solution)/shard_map/pallas_call | solution.py:478
  123.8 0.7 copy.9
  124.5 2.2 %copy.10 = bf16[1,3072,768]{2,1,0:T(8,128)(2,1)} copy(bf16[1,3072,768]{2,1,0:T(8,128)(2,1)S(1)} %bitcast.4) | data formatting | bytes 9437184
  126.7 0.6 copy.11
Async XLA Ops:
  0.6 0.9 copy-start
  1.6 0.7 copy-start.1

commit v4 on v3

--- a/solution.py
+++ b/solution.py
@@ -23,10 +23,10 @@
     leave_ref, grad_hbm, total_ref,
     w_ref, stage, standard, scale, resid, a_ref,
     part, part_out, part_in, hid_out, hid_in, carried,
-    y_own, y_out, y_in, ring_in, wg, tot, back, summed,
+    y_own, y_out, y_in, x_out, x_in, ring_in, wg, tot, back, summed,
     v_out, v_in,
     w_sem, wg_sem, group_s, group_r, resid_sem, ag_s, ag_r, sib_s, sib_r,
-    dp_s, dp_r, sec_s, sec_r, y_s, y_r, rs_s, rs_r, fin_s, fin_r,
+    dp_s, dp_r, sec_s, sec_r, share_s, share_r, y_s, y_r, x_s, x_r, rs_s, rs_r, fin_s, fin_r,
     v_s, v_r,
 ):
     sec = lax.axis_index("section")
@@ -173,84 +173,117 @@
         units += [((phase, NZ - k), (phase, k)) for phase in (0, 1)]
     units += [((0, 4), (1, 4))]
 
-    def mm1(u):
-        for phase, o in units[u]:
+    def blocks_of(group):
+        return [(phase, o, zblock(o)) for u in group for phase, o in units[u]]
+
+    def mm1(*group):
+        blocks = blocks_of(group)
+        for phase, o, _ in blocks:
             sib_wait(phase, o)
-        (p1, b1), (p2, b2) = [(phase, zblock(o)) for phase, o in units[u]]
 
         @pl.loop(0, width // 256)
         def _(n):
             cols = pl.ds(pl.multiple_of(n * 256, 256), 256)
             acc = None
             for q in range(2):
-                left = jnp.concatenate([a_ref[q, p1, b1], a_ref[q, p2, b2]], axis=0)
+                left = jnp.concatenate([a_ref[q, phase, b] for phase, _, b in blocks], axis=0)
                 d = jnp.dot(left, w_ref[q * quarter:(q + 1) * quarter, cols], preferred_element_type=F32)
                 acc = d if acc is None else acc + d
-            part[u, :, cols] = acc
-            part_out[u, :, cols] = acc.astype(BF)
-
-        start(copy(part_out.at[u], part_in.at[u], dp_s.at[u], dp_r.at[u], dp_mate))
+            for i, u in enumerate(group):
+                part[u, :, cols] = acc[i * 128:(i + 1) * 128]
+                part_out[u, :, cols] = acc[i * 128:(i + 1) * 128].astype(BF)
+
+        for u in group:
+            start(dp_copy(u))
+
+    def dp_copy(u):
+        theirs = pl.ds(pl.multiple_of((1 - rep) * 64, 64), 64)
+        return copy(part_out.at[u, theirs], part_in.at[u], dp_s.at[u], dp_r.at[u], dp_mate)
+
+    def sec_copy(u):
+        return copy(hid_out.at[u], hid_in.at[u], sec_s.at[u], sec_r.at[u], sec_mate)
+
+    def own_block(u):
+        (p1, o1), (p2, o2) = units[u]
+        return p1 + rep * (p2 - p1), zblock(o1 + rep * (o2 - o1))
+
+    def share_copy(u):
+        phase, b = own_block(u)
+        block = carried.at[phase, b]
+        return copy(block, block, share_s.at[u], share_r.at[u], dp_mate)
 
     def mid1(u):
-        copy(part_out.at[u], part_in.at[u], dp_s.at[u], dp_r.at[u], dp_mate).wait_recv()
+        dp_copy(u).wait_recv()
 
         @pl.when(leading)
         def _():
-            @pl.loop(0, 8)
+            @pl.loop(0, 4)
             def _(n):
                 rows = pl.ds(pl.multiple_of(n * 16, 16), 16)
-                p = part[u, rows, :] + part_in[u, rows, :].astype(F32)
+                mine = pl.ds(pl.multiple_of(rep * 64 + n * 16, 16), 16)
+                p = part[u, mine, :] + part_in[u, rows, :].astype(F32)
                 sq = p * p
                 inner = jnp.tanh(coeff * (p + 0.044715 * sq * p))
                 one = 1.0 + inner
                 hid_out[u, rows, :] = (0.5 * p * one).astype(BF)
-                part[u, rows, :] = 0.5 * one + 0.5 * p * (1.0 - inner * inner) * coeff * (
+                part[u, mine, :] = 0.5 * one + 0.5 * p * (1.0 - inner * inner) * coeff * (
                     1.0 + 3.0 * 0.044715 * sq
                 )
 
         @pl.when(jnp.logical_not(leading))
         def _():
-            @pl.loop(0, 8)
+            @pl.loop(0, 4)
             def _(n):
                 rows = pl.ds(pl.multiple_of(n * 16, 16), 16)
-                hid_out[u, rows, :] = (part[u, rows, :] + part_in[u, rows, :].astype(F32)).astype(BF)
-
-        start(copy(hid_out.at[u], hid_in.at[u], sec_s.at[u], sec_r.at[u], sec_mate))
+                mine = pl.ds(pl.multiple_of(rep * 64 + n * 16, 16), 16)
+                hid_out[u, rows, :] = (part[u, mine, :] + part_in[u, rows, :].astype(F32)).astype(BF)
+
+        start(sec_copy(u))
 
     def mid2(u):
-        copy(hid_out.at[u], hid_in.at[u], sec_s.at[u], sec_r.at[u], sec_mate).wait_recv()
-        for i, (phase, o) in enumerate(units[u]):
-            b = zblock(o)
-
-            @pl.when(leading)
-            def _():
-                @pl.loop(0, 4)
-                def _(n):
-                    src = pl.ds(pl.multiple_of(i * 64 + n * 16, 16), 16)
-                    dst = pl.ds(pl.multiple_of(n * 16, 16), 16)
-                    carried[phase, b, dst, :] = (hid_in[u, src, :].astype(F32) * part[u, src, :]).astype(BF)
-
-            @pl.when(jnp.logical_not(leading))
-            def _():
-                carried[phase, b] = hid_in[u, i * 64:(i + 1) * 64, :]
-
-    def mm2(u):
-        (p1, o1), (p2, o2) = units[u]
-        b1, b2 = zblock(o1), zblock(o2)
+        sec_copy(u).wait_recv()
+        phase, b = own_block(u)
+
+        @pl.when(leading)
+        def _():
+            @pl.loop(0, 4)
+            def _(n):
+                rows = pl.ds(pl.multiple_of(n * 16, 16), 16)
+                mine = pl.ds(pl.multiple_of(rep * 64 + n * 16, 16), 16)
+                carried[phase, b, rows, :] = (hid_in[u, rows, :].astype(F32) * part[u, mine, :]).astype(BF)
+
+        @pl.when(jnp.logical_not(leading))
+        def _():
+            carried[phase, b] = hid_in[u]
+
+        start(share_copy(u))
+
+    def mm2(*group):
+        for u in group:
+            share_copy(u).wait_recv()
+        blocks = blocks_of(group)
         for half, dst in ((1 - core, y_out), (core, y_own)):
             @pl.loop(0, quarter // 256)
             def _(n):
-                left = jnp.concatenate([carried[p1, b1], carried[p2, b2]], axis=0)
+                left = jnp.concatenate([carried[phase, b] for phase, _, b in blocks], axis=0)
                 right = w_ref[pl.ds(pl.multiple_of(half * quarter + n * 256, 256), 256), :]
-                d = lax.dot_general(
-                    left, right, (((1,), (1,)), ((), ())), preferred_element_type=F32
-                ).astype(BF)
+                d = lax.dot_general(left, right, (((1,), (1,)), ((), ())), preferred_element_type=F32)
                 cols = pl.ds(pl.multiple_of(n * 256, 256), 256)
-                dst[p1, o1, :, cols] = d[:64]
-                dst[p2, o2, :, cols] = d[64:]
+                for i, (phase, o, _) in enumerate(blocks):
+                    dst[phase, o, :, cols] = d[i * 64:(i + 1) * 64].astype(BF)
+
+                @pl.when(leading)
+                def _():
+                    line = None
+                    for i, (phase, _, b) in enumerate(blocks):
+                        term = d[i * 64:(i + 1) * 64] * a_ref[half, phase, b, :, cols].astype(F32)
+                        line = term if line is None else line + term
+                    line = jnp.sum(line, axis=0, keepdims=True)
+                    place = pl.ds(pl.multiple_of(half * quarter + n * 256, 256), 256)
+                    v_out[0, :, place] = line if group[0] == 0 else v_out[0, :, place] + line
 
             if dst is y_out:
-                for phase, o in units[u]:
+                for phase, o, _ in blocks:
                     start(copy(
                         y_out.at[phase, o], y_in.at[phase, o], y_s.at[phase, o], y_r.at[phase, o], sibling
                     ))
@@ -260,32 +293,62 @@
             y_out.at[phase, o], y_in.at[phase, o], y_s.at[phase, o], y_r.at[phase, o], sibling
         ).wait_recv()
 
+    third = quarter // 3
+    both = slice(0, third)
+    mine_to = slice(third, 2 * third)
+    mine_cols = pl.ds(pl.multiple_of(third + xlo * third, 128), third)
+    theirs_cols = pl.ds(pl.multiple_of(2 * third - xlo * third, 128), third)
+    ring_cols = slice(0, 2 * third)
+
+    def x_copy(phase, o):
+        return copy(x_out.at[phase, o], x_in.at[phase, o], x_s.at[phase, o], x_r.at[phase, o], doubling[1])
+
+    def x_step(phase, o):
+        y_wait(phase, o)
+
+        @pl.loop(0, 4)
+        def _(n):
+            rows = pl.ds(pl.multiple_of(n * 16, 16), 16)
+            x_out[phase, o, rows, :] = (
+                y_own[phase, o, rows, theirs_cols].astype(F32) + y_in[phase, o, rows, theirs_cols].astype(F32)
+            ).astype(BF)
+
+        start(x_copy(phase, o))
+
+    def block_sums(phase, o, rows):
+        common = y_own[phase, o, rows, both].astype(F32) + y_in[phase, o, rows, both].astype(F32)
+        own = y_own[phase, o, rows, mine_cols].astype(F32) + y_in[phase, o, rows, mine_cols].astype(F32)
+        return common, own + x_in[phase, o, rows, :].astype(F32)
+
     def rs_copy(phase, way, i):
         count = steps_of(phase, way)
         o = count - i if way == UP else NZ - (count - i)
         return o, copy(
-            y_own.at[phase, o], ring_in.at[phase, way, i], rs_s.at[phase, way, i], rs_r.at[phase, way, i],
+            y_own.at[phase, o, :, ring_cols], ring_in.at[phase, way, i],
+            rs_s.at[phase, way, i], rs_r.at[phase, way, i],
             above if way == UP else below,
         )
 
     def rs_step(phase, way, i):
         o, c = rs_copy(phase, way, i)
-        y_wait(phase, o)
+        x_copy(phase, o).wait_recv()
         if i:
             rs_copy(phase, way, i - 1)[1].wait_recv()
 
         @pl.loop(0, 4)
         def _(n):
             rows = pl.ds(pl.multiple_of(n * 16, 16), 16)
-            s = y_own[phase, o, rows, :].astype(F32) + y_in[phase, o, rows, :].astype(F32)
+            common, own = block_sums(phase, o, rows)
             if i:
-                s += ring_in[phase, way, i - 1, rows, :].astype(F32)
-            y_own[phase, o, rows, :] = s.astype(BF)
+                common += ring_in[phase, way, i - 1, rows, both].astype(F32)
+                own += ring_in[phase, way, i - 1, rows, mine_to].astype(F32)
+            y_own[phase, o, rows, both] = common.astype(BF)
+            y_own[phase, o, rows, mine_to] = own.astype(BF)
 
         start(c)
 
     def rs_final(phase):
-        y_wait(phase, 0)
+        x_copy(phase, 0).wait_recv()
         last = [steps_of(phase, way) - 1 for way in (UP, DOWN)]
         for way in (UP, DOWN):
             rs_copy(phase, way, last[way])[1].wait_recv()
@@ -293,10 +356,12 @@
         @pl.loop(0, 4)
         def _(n):
             rows = pl.ds(pl.multiple_of(n * 16, 16), 16)
-            s = y_own[phase, 0, rows, :].astype(F32) + y_in[phase, 0, rows, :].astype(F32)
+            common, own = block_sums(phase, 0, rows)
             for way in (UP, DOWN):
-                s += ring_in[phase, way, last[way], rows, :].astype(F32)
-            tot[phase, rows, :] = s.astype(BF)
+                common += ring_in[phase, way, last[way], rows, both].astype(F32)
+                own += ring_in[phase, way, last[way], rows, mine_to].astype(F32)
+            tot[phase, rows, both] = common.astype(BF)
+            tot[phase, rows, mine_to] = own.astype(BF)
 
         for o in range(4):
             xx = lax.rem(x + o, 4)
@@ -326,16 +391,6 @@
             rows = pl.ds(pl.multiple_of(t * 256, 256), 256)
             wg[rows, :] = d.astype(BF)
 
-            @pl.when(leading)
-            def _():
-                fold = jnp.zeros((256, 128), F32)
-                for m in range(width // 128):
-                    lanes = slice(m * 128, (m + 1) * 128)
-                    fold += d[:, lanes] * w_ref[rows, lanes].astype(F32)
-                line = jnp.sum(fold.T, axis=0, keepdims=True)
-                gains = vec_ref[:, pl.ds(pl.multiple_of(rep * half_model + t * 256, 256), 256)]
-                v_out[0, :, rows] = line / gains
-
         rows = pl.ds(first * 256, count * 256)
         c = pltpu.make_async_copy(wg.at[rows], grad_hbm.at[rows], wg_sem.at[len(copies)])
         c.start()
@@ -359,43 +414,45 @@
         sib_send(phase, 0)
     w_copy.wait()
     mm1(0)
-    for u in range(1, 8):
-        if u < 7:
-            forward((u - 1) % 2, (u + 1) // 2)
+    for j in range(1, 5):
+        forward(0, j)
+        forward(1, j)
+        if j == 1:
+            mm1(1, 2)
+            mid1(0)
+        elif j == 2:
+            mm1(3, 4)
+            mid2(0)
+            mid1(1)
+            mid1(2)
+        elif j == 3:
+            mm1(5, 6)
+            mid2(1)
+            mid2(2)
+            mid1(3)
+            mid1(4)
+            mm2(0)
         else:
-            forward(0, 4)
-            forward(1, 4)
-        mm1(u)
-        if u >= 2:
-            mid1(u - 2)
-        if u >= 4:
-            mid2(u - 4)
-        if u >= 5:
-            mm2(u - 5)
-    mid2(4)
-    mid1(6)
+            mm1(7)
+            mid2(3)
+            mid2(4)
+            mid1(5)
+            mid1(6)
+            mm2(1, 2)
+    mid1(7)
     mid2(5)
-    mm2(5)
-    rs_step(0, DOWN, 0)
-    mid1(7)
     mid2(6)
-    mm2(6)
-    rs_step(1, UP, 0)
-    mm2(3)
-    rs_step(0, DOWN, 1)
+    mm2(3, 4)
     mid2(7)
+    mm2(5, 6)
+    x_step(0, 5)
+    x_step(1, 3)
     mm2(7)
-    rs_step(0, UP, 0)
-    rs_step(1, DOWN, 0)
-    mm2(4)
-    rs_step(1, UP, 1)
-    rs_step(0, DOWN, 2)
-    rs_step(1, UP, 2)
-    per = model // 512 // 3
-    for i in range(1, 4):
-        wgrad((i - 1) * per, per)
-        rs_step(0, UP, i)
-        rs_step(1, DOWN, i)
+
+    @pl.when(leading)
+    def _():
+        gains = vec_ref[:, pl.ds(pl.multiple_of(rep * half_model, 128), half_model)]
+        v_out[0] = v_out[0] / gains
 
     @pl.when(jnp.logical_not(leading))
     def _():
@@ -407,11 +464,46 @@
             v_out[0, :, q * quarter:(q + 1) * quarter] = line
 
     start(vec_copy(0))
+    x_step(0, 4)
+    x_step(1, 4)
+    rs_step(0, DOWN, 0)
+    rs_step(1, UP, 0)
     vec_next(0)
+    x_step(0, 6)
+    x_step(1, 2)
+    rs_step(0, UP, 0)
+    rs_step(1, DOWN, 0)
+    x_step(0, 3)
+    x_step(1, 5)
+    rs_step(0, DOWN, 1)
+    rs_step(1, UP, 1)
+    vec_next(1)
+    x_step(0, 7)
+    x_step(1, 1)
+    wgrad(0, 2)
+    rs_step(0, UP, 1)
+    rs_step(1, DOWN, 1)
+    x_step(0, 2)
+    x_step(1, 6)
+    rs_step(0, DOWN, 2)
+    rs_step(1, UP, 2)
+    vec_next(2)
+    x_step(0, 1)
+    x_step(1, 7)
+    wgrad(2, 2)
+    rs_step(0, UP, 2)
+    rs_step(1, DOWN, 2)
+    vec_next(3)
+    x_step(0, 0)
+    x_step(1, 0)
+    wgrad(4, 2)
+    rs_step(0, UP, 3)
+    rs_step(1, DOWN, 3)
+    vec_next(4)
+    wgrad(6, 3)
     rs_final(0)
     rs_final(1)
-    vec_next(1)
-    vec_next(2)
+    wgrad(9, 3)
 
     copy(rows_ref, resid, resid_sem.at[0], resid_sem.at[1], sec_mate).wait_recv()
     for o in range(1, 8):
@@ -420,7 +512,11 @@
 
     def quarter_sum(q):
         j = (q // 2) * 4 + q % 2
-        return back[j].astype(F32) + back[j + 2].astype(F32)
+        return jnp.concatenate([
+            back[j, :, both].astype(F32) + back[j + 2, :, both].astype(F32),
+            back[j, :, mine_to].astype(F32),
+            back[j + 2, :, mine_to].astype(F32),
+        ], axis=1)
 
     @pl.when(leading)
     def _():
@@ -448,8 +544,6 @@
             cols = slice(q * quarter, (q + 1) * quarter)
             leave_ref[:, cols] = (resid[:, cols].astype(F32) + quarter_sum(q) + vec_ref[:, cols]).astype(BF)
 
-    vec_next(3)
-    vec_next(4)
     vec_copy(5).wait_recv()
     mine = pl.ds(pl.multiple_of(rep * half_model, 128), half_model)
     other = pl.ds(pl.multiple_of((1 - rep) * half_model, 128), half_model)
@@ -475,6 +569,7 @@
     dma = pltpu.SemaphoreType.DMA
     vm = pltpu.VMEM
     block = (64, quarter)
+    third = quarter // 3
     leaving, weight_grad, totals = pl.pallas_call(
         kernel,
         out_shape=(
@@ -501,24 +596,26 @@
             vm((2, 2, NZ, *block), BF),
             vm((8, 128, width), F32),
             vm((8, 128, width), BF),
-            vm((8, 128, width), BF),
-            vm((8, 128, width), BF),
-            vm((8, 128, width), BF),
+            vm((8, 64, width), BF),
+            vm((8, 64, width), BF),
+            vm((8, 64, width), BF),
             vm((2, NZ, 64, width), BF),
             vm((2, NZ, *block), BF),
             vm((2, NZ, *block), BF),
             vm((2, NZ, *block), BF),
-            vm((2, 2, 4, *block), BF),
+            vm((2, NZ, 64, third), BF),
+            vm((2, NZ, 64, third), BF),
+            vm((2, 2, 4, 64, 2 * third), BF),
             vm((half, width), BF),
-            vm((2, *block), BF),
-            vm((8, 16, quarter), BF),
+            vm((2, 64, 2 * third), BF),
+            vm((8, 16, 2 * third), BF),
             vm((16, model), F32),
             vm((6, 1, half), F32),
             vm((6, 1, half), F32),
-            dma, dma((4,)), dma((8,)), dma((8,)), dma((2,)),
+            dma, dma((5,)), dma((8,)), dma((8,)), dma((2,)),
             dma((2, 2, 4)), dma((2, 2, 4)), dma((2, NZ)), dma((2, NZ)),
-            dma((8,)), dma((8,)), dma((8,)), dma((8,)),
-            dma((2, NZ)), dma((2, NZ)), dma((2, 2, 4)), dma((2, 2, 4)),
+            dma((8,)), dma((8,)), dma((8,)), dma((8,)), dma((8,)), dma((8,)),
+            dma((2, NZ)), dma((2, NZ)), dma((2, NZ)), dma((2, NZ)), dma((2, 2, 4)), dma((2, 2, 4)),
             dma((2, 4)), dma((8,)),
             dma((6,)), dma((6,)),
         ],

time: 129 us -> 116 us (0.90); the launches traced: 127 us -> 116 us
  Pallas kernels: 122 us -> 110 us
    pallas_call x1, Pallas kernels: 122 us -> 110 us  [local(): pl.pallas_call(kernel, out_shape=(jax.ShapeDtypeStruct((micro * rows, mod...]
where the time goes in v4:
time: 116 us
  Pallas kernels  110 us (95%)
  local copies, waits for them, and re-layouts  5.13 us (4%)
    pallas_call x1, Pallas kernels, local(): pl.pallas_call(kernel, out_shape=(jax.ShapeDtypeStruct((micro * rows, mod...  110 us
    unnamed x7, local copies, waits for them, and re-layouts  5.13 us

profile of v4, /device:TPU:1, one launch (start us, length us, event | category | flops | bytes accessed | tf_op | source)
XLA Modules:
  0.0 116.0 jit_solution(10994949111376234506)
XLA Ops:
  0.6 0.0 copy-start
  0.6 0.9 copy-done
  1.6 0.0 copy-start.1
  1.6 0.7 copy-done.1
  2.3 110.2 %shard_map.58 = (bf16[16,6144]{1,0:T(8,128)(2,1)S(1)}, bf16[3072,768]{1,0:T(8,128)(2,1)S(1)}, f32[1,6144]{1,0:T(1,128)S(1)}) custom-call(bf16[3072,768]{1,0:T(8,128)(2,1)} %bitcast.7, bf16[16,6144]{1,0:T(8,128)(2,1)S(1)} %bitcast.6, f32[1,6144]{1,0:T(1,128)S(1)} %copy-done.1), custom_call_target="tpu_custom_call" | custom-call | flops 14495514624 | bytes 9437184 | tf_op jit(solution)/shard_map/pallas_call | solution.py:573
  112.5 0.7 copy.9
  113.2 2.2 %copy.10 = bf16[1,3072,768]{2,1,0:T(8,128)(2,1)} copy(bf16[1,3072,768]{2,1,0:T(8,128)(2,1)S(1)} %bitcast.4) | data formatting | bytes 9437184
  115.4 0.6 copy.11
Async XLA Ops:
  0.6 0.9 copy-start
  1.6 0.7 copy-start.1

commit v5 on v4

--- a/solution.py
+++ b/solution.py
@@ -434,10 +434,10 @@
             mm2(0)
         else:
             mm1(7)
+            mid1(5)
+            mid1(6)
             mid2(3)
             mid2(4)
-            mid1(5)
-            mid1(6)
             mm2(1, 2)
     mid1(7)
     mid2(5)

time: 116 us -> 116 us (level)
  no operation moved by 1% of the time
where the time goes in v5:
time: 116 us
  Pallas kernels  110 us (95%)
  local copies, waits for them, and re-layouts  5.13 us (4%)
    pallas_call x1, Pallas kernels, local(): pl.pallas_call(kernel, out_shape=(jax.ShapeDtypeStruct((micro * rows, mod...  110 us
    unnamed x7, local copies, waits for them, and re-layouts  5.13 us

profile of v5, /device:TPU:1, one launch (start us, length us, event | category | flops | bytes accessed | tf_op | source)
XLA Modules:
  0.0 116.0 jit_solution(12527654361777413574)
XLA Ops:
  0.6 0.0 copy-start
  0.6 0.9 copy-done
  1.6 0.0 copy-start.1
  1.6 0.7 copy-done.1
  2.3 110.2 %shard_map.58 = (bf16[16,6144]{1,0:T(8,128)(2,1)S(1)}, bf16[3072,768]{1,0:T(8,128)(2,1)S(1)}, f32[1,6144]{1,0:T(1,128)S(1)}) custom-call(bf16[3072,768]{1,0:T(8,128)(2,1)} %bitcast.7, bf16[16,6144]{1,0:T(8,128)(2,1)S(1)} %bitcast.6, f32[1,6144]{1,0:T(1,128)S(1)} %copy-done.1), custom_call_target="tpu_custom_call" | custom-call | flops 14495514624 | bytes 9437184 | tf_op jit(solution)/shard_map/pallas_call | solution.py:573
  112.5 0.7 copy.9
  113.2 2.2 %copy.10 = bf16[1,3072,768]{2,1,0:T(8,128)(2,1)} copy(bf16[1,3072,768]{2,1,0:T(8,128)(2,1)S(1)} %bitcast.4) | data formatting | bytes 9437184
  115.4 0.6 copy.11
Async XLA Ops:
  0.6 0.9 copy-start
  1.6 0.7 copy-start.1
